TPU v7x, 256 devices: a whole 4x4x8 slice. The times are simulated.
256 devices in a mesh: space: 16 (over y, x), tblock: 16 (over z, core).
Axes of the slice: x: 4, y: 4, z: 8, core: 2. Of those that a mesh axis runs over, the one named last changes fastest.
Arguments:
- snapshots: bfloat16 [16, 256, 3, 106496], P('tblock', None, None, 'space'), may hold values from -70 to 70
Outputs:
- modes: bfloat16 [128, 2, 4, 3, 106496], P('tblock', None, None, None, 'space')
- energies: float32 [128, 4], P('tblock')
All inputs are finite; a program needn't handle non-finite values.
Results may differ from a plain program's by a relative error of at most 0.0085.
Values may be sent and summed in bfloat16 or wider, within the bound.
A program may use at most 128 MiB of HBM per device.

v0:
```python
import math

import jax
import jax.numpy as jnp
from jax import lax
from jax.sharding import PartitionSpec as P

MODES = 4
SUBSPACE_ITERS = 6


def spectral_table(step_count):
    times = jnp.arange(step_count, dtype=jnp.int32)
    orders = jnp.arange(1, step_count // 2 + 1, dtype=jnp.int32)
    phase = orders[:, None] * times[None, :] % step_count
    angle = 2.0 * math.pi / step_count * phase.astype(jnp.float32)
    window = 0.5 - 0.5 * jnp.cos(2.0 * math.pi / step_count * times.astype(jnp.float32))
    scaled = window / math.sqrt(0.375 * step_count)
    rows = jnp.stack([scaled * jnp.cos(angle), -scaled * jnp.sin(angle)], axis=1)
    return rows.reshape(step_count, step_count).astype(jnp.bfloat16)


def batch_mult(left, right):
    return jnp.einsum("fbe,fek->fbk", left, right, precision=lax.Precision.HIGHEST)


def apply_gram(gram_real, gram_imag, vec_real, vec_imag):
    out_real = batch_mult(gram_real, vec_real) - batch_mult(gram_imag, vec_imag)
    out_imag = batch_mult(gram_real, vec_imag) + batch_mult(gram_imag, vec_real)
    return (out_real, out_imag)


def orthonormal(wide_real, wide_imag):
    done_real = []
    done_imag = []
    for column in range(wide_real.shape[2]):
        vec_real = wide_real[:, :, column]
        vec_imag = wide_imag[:, :, column]
        for earlier in range(column):
            base_real = done_real[earlier]
            base_imag = done_imag[earlier]
            proj_real = jnp.sum(base_real * vec_real + base_imag * vec_imag, axis=1, keepdims=True)
            proj_imag = jnp.sum(base_real * vec_imag - base_imag * vec_real, axis=1, keepdims=True)
            vec_real = vec_real - (base_real * proj_real - base_imag * proj_imag)
            vec_imag = vec_imag - (base_real * proj_imag + base_imag * proj_real)
        length = jnp.sqrt(jnp.sum(vec_real * vec_real + vec_imag * vec_imag, axis=1, keepdims=True))
        done_real.append(vec_real / length)
        done_imag.append(vec_imag / length)
    return (jnp.stack(done_real, axis=2), jnp.stack(done_imag, axis=2))


def leading_modes(gram_real, gram_imag):
    freq_count, block_count = (gram_real.shape[0], gram_real.shape[1])
    basis = jnp.eye(block_count, MODES, dtype=jnp.float32)
    vec_real = jnp.broadcast_to(basis[None], (freq_count, block_count, MODES))
    vec_imag = jnp.zeros((freq_count, block_count, MODES), jnp.float32)
    for sweep in range(SUBSPACE_ITERS):
        wide_real, wide_imag = apply_gram(gram_real, gram_imag, vec_real, vec_imag)
        vec_real, vec_imag = orthonormal(wide_real, wide_imag)
    wide_real, wide_imag = apply_gram(gram_real, gram_imag, vec_real, vec_imag)
    energy = jnp.sum(vec_real * wide_real + vec_imag * wide_imag, axis=1)
    scale = 1.0 / jnp.sqrt(energy)
    amp_real = jnp.transpose(vec_real, (0, 2, 1)) * scale[:, :, None]
    amp_imag = jnp.transpose(vec_imag, (0, 2, 1)) * scale[:, :, None]
    first = jnp.stack([amp_real, -amp_imag], axis=2)
    second = jnp.stack([amp_imag, amp_real], axis=2)
    coef = jnp.stack([first, second], axis=1).astype(jnp.bfloat16)
    return (coef, energy)


def local(snapshots):
    step_count = snapshots.shape[1]
    comp_count = snapshots.shape[2]
    point_count = snapshots.shape[3]
    width = comp_count * point_count
    half_count = step_count // 2
    dft_table = spectral_table(step_count)
    series = snapshots.reshape(step_count, width)
    spectra = jnp.dot(dft_table, series, preferred_element_type=jnp.float32).astype(jnp.bfloat16)
    spectra = spectra.reshape(half_count, 2, 1, width)
    mine = lax.all_to_all(spectra, "tblock", split_axis=0, concat_axis=2, tiled=True)
    partial_sums = jnp.einsum("frbx,fsex->frsbe", mine, mine, preferred_element_type=jnp.float32)
    local_bins = mine.shape[0]
    totals = lax.psum(partial_sums, "space")
    products = totals / (3.0 * point_count * lax.axis_size("space"))
    gram_real = products[:, 0, 0] + products[:, 1, 1]
    gram_imag = products[:, 0, 1] - products[:, 1, 0]
    coef, energies = leading_modes(gram_real, gram_imag)
    modes = jnp.einsum("fojrb,frbx->fojx", coef, mine, preferred_element_type=jnp.float32).astype(
        jnp.bfloat16
    )
    modes = modes.reshape(local_bins, 2, MODES, comp_count, point_count)
    return (modes, energies)


def solution(mesh):
    in_specs = (P("tblock", None, None, "space"),)
    out_specs = (P("tblock", None, None, None, "space"), P("tblock", None))
    return jax.shard_map(local, mesh=mesh, in_specs=in_specs, out_specs=out_specs, check_vma=False)
```

profile of v0, /device:TPU:32, one launch (start us, length us, event | category | flops | bytes accessed | tf_op | source)
XLA Modules:
  0.0 397.6 jit_solution(5097667462006772650)
XLA Ops:
  0.7 0.6 multiply_convert_fusion.1
  1.5 14.3 %copy.196 = bf16[1,256,3,6656]{1,3,2,0:T(8,128)(2,1)} copy(bf16[1,256,3,6656]{3,1,2,0:T(8,128)(2,1)} %param.1) | data formatting | bytes 20447232 | tf_op args[0]
  15.8 13.0 %convolution_convert_fusion = bf16[256,19968]{1,0:T(8,128)(2,1)} fusion(bf16[256,256]{1,0:T(8,128)(2,1)S(1)} %convert_element_type.56, bf16[256,19968]{0,1:T(8,128)(2,1)} %bitcast.909), kind=kOutput, calls=%fused_computation | convolution fusion | flops 2622357504 | bytes 20578304 | tf_op jit(solution)/shard_map/dot_general | solution.py:79
  28.9 14.2 %reshape.3258 = bf16[128,2,1,19968]{3,1,0,2:T(2,128)(2,1)} reshape(bf16[256,19968]{1,0:T(8,128)(2,1)} %convolution_convert_fusion) | data formatting | bytes 20447232 | tf_op jit(solution)/shard_map/reshape | solution.py:80
  43.1 8.6 %all-to-all-start = ((bf16[128,2,1,19968]{3,1,2,0:T(2,128)(2,1)}), bf16[128,2,1,19968]{3,1,2,0:T(2,128)(2,1)}, u32[]{:S(2)}, u32[]{:S(2)}) async-start(bf16[128,2,1,19968]{3,1,2,0:T(2,128)(2,1)} %bitcast.908), calls=%async_computation | async-start | bytes 20447232 | tf_op jit(solution)/shard_map/all_to_all | solution.py:81
  51.7 222.3 %all-to-all-done = bf16[128,2,1,19968]{3,1,2,0:T(2,128)(2,1)} async-done(((bf16[128,2,1,19968]{3,1,2,0:T(2,128)(2,1)}), bf16[128,2,1,19968]{3,1,2,0:T(2,128)(2,1)}, u32[]{:S(2)}, u32[]{:S(2)}) %all-to-all-start) | async-done | bytes 10223648 | tf_op jit(solution)/shard_map/all_to_all | solution.py:81
  273.9 18.6 %fusion.7 = f32[8,2,2,16,16]{3,4,1,2,0:T(8,128)S(1)} fusion(bf16[16,8,2,1,19968]{4,2,1,0,3:T(2,128)(2,1)} %bitcast.2), kind=kOutput, calls=%fused_computation.9 | convolution fusion | flops 327155712 | bytes 10256384 | tf_op jit(solution)/shard_map/frbx,fsex->frsbe/dot_general | solution.py:82
  292.5 77.2 %psum.7 = f32[8,2,2,16,16]{3,4,1,2,0:T(8,128)S(1)} all-reduce(f32[8,2,2,16,16]{3,4,1,2,0:T(8,128)S(1)} %fusion.7), channel_id=1, replica_groups=mesh['space'=16,'tblock'=16] {'space'}, use_global_device_ids=true, to_apply=%region_0.1 | all-reduce | flops 8192 | bytes 65536 | tf_op jit(solution)/shard_map/psum | solution.py:84
  370.7 0.3 fusion.159
  371.0 0.2 add_reduce_fusion.35
  371.2 0.2 add_reduce_fusion.32
  371.4 0.2 add_reduce_fusion.33
  371.6 0.2 add_reduce_fusion.31
  371.9 0.2 add_reduce_fusion.30
  372.2 0.2 fusion.67
  372.4 0.2 fusion.65
  372.7 0.2 fusion.71
  372.9 0.2 fusion.69
  373.2 0.3 fusion.145
  373.5 0.2 add_reduce_fusion.29
  373.7 0.2 add_reduce_fusion.26
  373.9 0.2 add_reduce_fusion.27
  374.1 0.2 add_reduce_fusion.25
  374.3 0.2 add_reduce_fusion.24
  374.6 0.2 fusion.59
  374.8 0.2 fusion.57
  375.1 0.2 fusion.63
  375.3 0.2 fusion.61
  375.7 0.3 fusion.131
  375.9 0.2 add_reduce_fusion.23
  376.2 0.2 add_reduce_fusion.20
  376.4 0.2 add_reduce_fusion.21
  376.6 0.2 add_reduce_fusion.19
  376.8 0.2 add_reduce_fusion.18
  377.1 0.2 fusion.51
  377.6 0.2 fusion.55
  377.8 0.2 fusion.53
  378.2 0.3 fusion.117
  378.4 0.2 add_reduce_fusion.17
  378.6 0.2 add_reduce_fusion.14
  378.9 0.2 add_reduce_fusion.15
  379.1 0.2 add_reduce_fusion.13
  379.3 0.2 add_reduce_fusion.12
  379.6 0.2 fusion.43
  379.8 0.2 fusion.41
  380.1 0.2 fusion.47
  380.3 0.2 fusion.45
  380.6 0.3 fusion.103
  380.9 0.2 add_reduce_fusion.11
  381.1 0.2 add_reduce_fusion.8
  381.4 0.2 add_reduce_fusion.9
  381.6 0.2 add_reduce_fusion.7
  381.8 0.2 add_reduce_fusion.6
  382.1 0.2 fusion.35
  382.3 0.2 fusion.33
  382.6 0.2 fusion.39
  382.8 0.2 fusion.37
  383.1 0.3 fusion.89
  383.4 0.2 add_reduce_fusion.5
  383.6 0.2 add_reduce_fusion.2
  383.8 0.2 add_reduce_fusion.3
  384.0 0.2 add_reduce_fusion.1
  385.0 0.2 fusion.31
  385.8 11.8 %fusion = bf16[8,2,4,19968]{3,2,1,0:T(4,128)(2,1)} fusion(bf16[16,8,2,1,19968]{4,2,1,0,3:T(2,128)(2,1)} %bitcast.2, bf16[8,2,4,2,16]{4,0,2,3,1:T(8,128)(2,1)S(1)} %pad_maximum_fusion.1), kind=kOutput, calls=%fused_computation.2 | convolution fusion | flops 83066880 | bytes 12783616 | tf_op jit(solution)/shard_map/fojrb,frbx->fojx/dot_general | solution.py:89
  (92 shorter events, 4.5 us)
Async XLA Ops:
  43.1 230.8 %all-to-all-start = ((bf16[128,2,1,19968]{3,1,2,0:T(2,128)(2,1)}), bf16[128,2,1,19968]{3,1,2,0:T(2,128)(2,1)}, u32[]{:S(2)}, u32[]{:S(2)}) async-start(bf16[128,2,1,19968]{3,1,2,0:T(2,128)(2,1)} %bitcast.908), calls=%async_computation | async-start | bytes 20447232 | tf_op jit(solution)/shard_map/all_to_all | solution.py:81
  385.5 12.1 %copy-start = (f32[8,4]{0,1:T(4,128)}, f32[8,4]{0,1:T(4,128)S(1)}, u32[]{:S(2)}) copy-start(f32[8,4]{0,1:T(4,128)S(1)} %fusion.23) | copy-start | bytes 388
where the time goes:
time: 399 us; the launch traced here: 398 us
  waiting for transfers between devices  222 us (56%)
  blocking collectives  77.2 us (19%)
  matrix products  48.7 us (12%)
  local copies, waits for them, and re-layouts  29 us (7%)
  other arithmetic  10.5 us (3%)
  starting transfers between devices  8.59 us (2%)
    all_to_all x1, waiting for transfers between devices, local(): lax.all_to_all(spectra, 'tblock', split_axis=0, concat_axis=2, tiled=True)  222 us
    psum x1, blocking collectives, local(): totals = lax.psum(partial_sums, 'space')  77.2 us
    dot_general x1, matrix products, local(): jnp.einsum('frbx,fsex->frsbe', mine, mine, preferred_element_type=jnp.flo...  18.6 us
    unnamed x4, local copies, waits for them, and re-layouts  14.4 us
    reshape x1, local copies, waits for them, and re-layouts, local(): spectra = spectra.reshape(half_count, 2, 1, width)  14.2 us
    dot_general x1, matrix products, local(): jnp.dot(dft_table, series, preferred_element_type=jnp.float32)  13 us
    dot_general x1, matrix products, local(): jnp.einsum('fojrb,frbx->fojx', coef, mine, preferred_element_type=jnp.flo...  11.8 us
    all_to_all x1, starting transfers between devices, local(): lax.all_to_all(spectra, 'tblock', split_axis=0, concat_axis=2, tiled=True)  8.59 us
  transfers between devices with their start and end apart: 1, of which 1 were waited for; matrix products, arithmetic and copies ran while one was open for 0% of the time, Pallas kernels for 0%

commit v1 on v0

v1 whole, which is shorter than its diff:
```python
import functools
import math

import jax
import jax.numpy as jnp
import numpy as np
from jax import lax
from jax.experimental import pallas as pl
from jax.experimental.pallas import tpu as pltpu
from jax.sharding import PartitionSpec as P

MODES = 4
SUBSPACE_ITERS = 6
BLOCKS = 16
STEPS = 256
BINS = 8
ROWS = 2 * BINS
COMPS = 3
CUTS = 4
LANES = 128
MESH = pl.DeviceIdType.MESH
VMEM_BYTES = 56 * 2**20


def spectral_table():
    times = np.arange(STEPS, dtype=np.int32)
    orders = np.arange(1, STEPS // 2 + 1, dtype=np.int32)
    phase = orders[:, None] * times[None, :] % STEPS
    angle = np.float32(2.0 * math.pi / STEPS) * phase.astype(np.float32)
    swing = np.cos(np.float32(2.0 * math.pi / STEPS) * times.astype(np.float32))
    window = np.float32(0.5) - np.float32(0.5) * swing
    scaled = window / np.float32(math.sqrt(0.375 * STEPS))
    rows = np.stack([scaled * np.cos(angle), -scaled * np.sin(angle)], axis=1)
    return jnp.asarray(rows.reshape(STEPS, STEPS).astype(np.float32)).astype(jnp.bfloat16)


def pack_gram(total):
    width = total.shape[1]
    cube = total.reshape(BLOCKS, ROWS, width)
    row = lax.broadcasted_iota(jnp.int32, (ROWS, width), 0)
    lane = lax.broadcasted_iota(jnp.int32, (ROWS, width), 1) % ROWS
    same_bin = row // 2 == lane // 2
    same_part = row % 2 == lane % 2
    first = jnp.where(same_bin & same_part, 1.0, 0.0)
    other = jnp.where(same_bin & (row % 2 < lane % 2), 1.0, 0.0)
    other = jnp.where(same_bin & (row % 2 > lane % 2), -1.0, other)
    real = jnp.sum(cube * first[None], axis=1)
    imag = jnp.sum(cube * other[None], axis=1)
    even = lax.broadcasted_iota(jnp.int32, (BLOCKS, width), 1) % 2 == 0
    real = real + pltpu.roll(real, width - 1, 1)
    imag = imag + pltpu.roll(imag, 1, 1)
    return jnp.where(even, real, imag)


def column_sum(value):
    return jnp.sum(value, axis=0, keepdims=True)


def leading_modes(packed, gram_ref):
    even = lax.broadcasted_iota(jnp.int32, (BLOCKS, LANES), 1) % 2 == 0
    per_half = LANES // ROWS
    for half in range(2):
        part = packed[:, half * LANES : (half + 1) * LANES]
        real = jnp.where(even, part, pltpu.roll(part, 1, 1))
        imag = jnp.where(even, pltpu.roll(part, LANES - 1, 1), part)
        for near in range(per_half):
            shift = (LANES - ROWS * near) % LANES
            block = half * per_half + near
            gram_ref[0, block] = real if shift == 0 else pltpu.roll(real, shift, 1)
            gram_ref[1, block] = imag if shift == 0 else pltpu.roll(imag, shift, 1)

    def apply_gram(vec_real, vec_imag):
        out_real = [None] * MODES
        out_imag = [None] * MODES
        for block in range(BLOCKS):
            real = gram_ref[0, block]
            imag = gram_ref[1, block]
            for j in range(MODES):
                row_real = vec_real[j][block : block + 1]
                row_imag = vec_imag[j][block : block + 1]
                term_real = real * row_real - imag * row_imag
                term_imag = real * row_imag + imag * row_real
                out_real[j] = term_real if block == 0 else out_real[j] + term_real
                out_imag[j] = term_imag if block == 0 else out_imag[j] + term_imag
        return out_real, out_imag

    def orthonormal(vec_real, vec_imag):
        vec_real = list(vec_real)
        vec_imag = list(vec_imag)
        for i in range(MODES):
            base_real = vec_real[i]
            base_imag = vec_imag[i]
            square = column_sum(base_real * base_real + base_imag * base_imag)
            inverse = 1.0 / square
            for j in range(i + 1, MODES):
                proj_real = column_sum(base_real * vec_real[j] + base_imag * vec_imag[j]) * inverse
                proj_imag = column_sum(base_real * vec_imag[j] - base_imag * vec_real[j]) * inverse
                vec_real[j] = vec_real[j] - (base_real * proj_real - base_imag * proj_imag)
                vec_imag[j] = vec_imag[j] - (base_real * proj_imag + base_imag * proj_real)
            scale = lax.rsqrt(square)
            vec_real[i] = base_real * scale
            vec_imag[i] = base_imag * scale
        return vec_real, vec_imag

    wide_real = [gram_ref[0, j] for j in range(MODES)]
    wide_imag = [gram_ref[1, j] for j in range(MODES)]
    vec_real, vec_imag = orthonormal(wide_real, wide_imag)

    def sweep(_, carry):
        return orthonormal(*apply_gram(*carry))

    vec_real, vec_imag = lax.fori_loop(1, SUBSPACE_ITERS, sweep, (vec_real, vec_imag))
    wide_real, wide_imag = apply_gram(vec_real, vec_imag)
    energies = [
        column_sum(vec_real[j] * wide_real[j] + vec_imag[j] * wide_imag[j]) for j in range(MODES)
    ]
    return vec_real, vec_imag, energies


def coefficient_matrix(vec_real, vec_imag, energies, order_ref):
    lane = lax.broadcasted_iota(jnp.int32, (BLOCKS, LANES), 1)
    even = lane % 2 == 0
    first = jnp.zeros((BLOCKS, LANES), jnp.float32)
    second = jnp.zeros((BLOCKS, LANES), jnp.float32)
    for j in range(MODES):
        scale = 1.0 / jnp.sqrt(energies[j])
        amp_real = vec_real[j] * scale
        amp_imag = vec_imag[j] * scale
        on_real = jnp.where(even, amp_real, amp_imag)
        on_imag = jnp.where(even, -amp_imag, amp_real)
        if j:
            on_real = pltpu.roll(on_real, ROWS * j, 1)
            on_imag = pltpu.roll(on_imag, ROWS * j, 1)
        here = lane // ROWS == j
        first = jnp.where(here, on_real, first)
        second = jnp.where(here, on_imag, second)
    shape = (BLOCKS, ROWS, LANES)
    row = lax.broadcasted_iota(jnp.int32, shape, 1)
    column = lax.broadcasted_iota(jnp.int32, shape, 2)
    whole = jnp.where(
        row % 2 == 0,
        jnp.broadcast_to(first[:, None, :], shape),
        jnp.broadcast_to(second[:, None, :], shape),
    )
    whole = jnp.where(row // 2 == column % ROWS // 2, whole, 0.0)
    turned = whole.reshape(BLOCKS * ROWS, LANES).T
    for j in range(MODES):
        for half in range(2):
            piece = turned[ROWS * j : ROWS * (j + 1), half * LANES : (half + 1) * LANES]
            order_ref[half, pl.ds(j, ROWS, stride=MODES), :] = piece
    return jnp.concatenate([order_ref[0], order_ref[1]], axis=1).astype(jnp.bfloat16)


def spectra_kernel(
    cut,
    scale,
    table_ref,
    series_ref,
    mine_ref,
    coef_ref,
    energy_ref,
    taken_ref,
    made_ref,
    total_ref,
    packed_ref,
    gram_ref,
    order_ref,
    take_sem,
    send_sem,
    recv_sem,
    sum_send_sem,
    sum_recv_sem,
):
    chunks = COMPS * CUTS
    here = lax.axis_index("space")
    me = lax.axis_index("tblock")
    level = me // 2
    core = lax.rem(me, 2)

    def peer(dz, dc):
        return lax.rem(level + dz, 8) * 2 + lax.rem(core + dc, 2)

    peers = [(dz, dc) for dz in (4, 3, 5, 2, 6, 1, 7, 0) for dc in (0, 1)][:-2] + [(0, 1)]

    barrier = pltpu.get_barrier_semaphore()
    for dz, dc in peers:
        pl.semaphore_signal(barrier, inc=1, device_id={"tblock": peer(dz, dc)}, device_id_type=MESH)
    for d in range(1, 16):
        pl.semaphore_signal(
            barrier, inc=1, device_id={"space": lax.rem(here + d, 16)}, device_id_type=MESH
        )

    def take(k):
        comp = k // CUTS
        start = pl.multiple_of(lax.rem(k, CUTS) * cut, LANES)
        slot = lax.rem(k, 2)
        return pltpu.make_async_copy(
            series_ref.at[comp, :, pl.ds(start, cut)], taken_ref.at[slot], take_sem.at[slot]
        )

    def send(k, dz, dc):
        to = peer(dz, dc)
        return pltpu.make_async_remote_copy(
            src_ref=made_ref.at[k, to],
            dst_ref=mine_ref.at[k, me],
            send_sem=send_sem.at[k, to],
            recv_sem=recv_sem.at[k, me],
            device_id={"tblock": to},
            device_id_type=MESH,
        )

    def arrival(k, dz, dc):
        sender = peer(dz, dc)
        return pltpu.make_async_remote_copy(
            src_ref=made_ref.at[k, sender],
            dst_ref=mine_ref.at[k, sender],
            send_sem=send_sem.at[k, sender],
            recv_sem=recv_sem.at[k, sender],
            device_id={"tblock": sender},
            device_id_type=MESH,
        )

    def make(k):
        take(k).wait()
        spectra = jnp.dot(
            table_ref[...], taken_ref[lax.rem(k, 2)], preferred_element_type=jnp.float32
        )
        made_ref[k] = spectra.astype(jnp.bfloat16).reshape(BLOCKS, ROWS, cut)
        mine_ref[k, me] = made_ref[k, me]

    take(0).start()
    take(1).start()
    make(0)
    pl.semaphore_wait(barrier, 30)
    for dz, dc in peers:
        send(0, dz, dc).start()

    def make_and_send(k, carry):
        @pl.when(k + 1 < chunks)
        def _():
            take(k + 1).start()

        make(k)
        for dz, dc in peers:
            send(k, dz, dc).start()
        return carry

    lax.fori_loop(1, chunks, make_and_send, 0)

    total_ref[...] = jnp.zeros_like(total_ref)

    def gather(k, carry):
        for dz, dc in peers:
            arrival(k, dz, dc).wait_recv()
        rows = mine_ref[k].reshape(BLOCKS * ROWS, cut)
        total_ref[...] += lax.dot_general(
            rows, rows, (((1,), (1,)), ((), ())), preferred_element_type=jnp.float32
        )
        return carry

    lax.fori_loop(0, chunks, gather, 0)

    packed_ref[here] = pack_gram(total_ref[...])

    def exchange(d, arriving):
        other = lax.rem(here + d, 16)
        slot = other if arriving else here
        return pltpu.make_async_remote_copy(
            src_ref=packed_ref.at[here],
            dst_ref=packed_ref.at[slot],
            send_sem=sum_send_sem.at[other],
            recv_sem=sum_recv_sem.at[slot],
            device_id={"space": other},
            device_id_type=MESH,
        )

    for d in range(1, 16):
        exchange(d, False).start()
    for d in range(1, 16):
        exchange(d, True).wait_recv()
    packed = packed_ref[0]
    for s in range(1, 16):
        packed = packed + packed_ref[s]
    packed = packed / scale

    vec_real, vec_imag, energies = leading_modes(packed, gram_ref)
    coef_ref[...] = coefficient_matrix(vec_real, vec_imag, energies, order_ref)
    wide = jnp.concatenate(energies, axis=0)
    lane = lax.broadcasted_iota(jnp.int32, (MODES, LANES), 1)
    narrow = wide
    for f in range(1, BINS):
        narrow = jnp.where(lane == f, pltpu.roll(wide, LANES - f, 1), narrow)
    energy_ref[...] = narrow[:, :BINS]

    def finish(k, carry):
        for dz, dc in peers:
            send(k, dz, dc).wait_send()
        return carry

    lax.fori_loop(0, chunks, finish, 0)
    for d in range(1, 16):
        exchange(d, False).wait_send()


def modes_kernel(coef_ref, mine_ref, out_ref):
    k = pl.program_id(0)
    rows = mine_ref[k].reshape(BLOCKS * ROWS, mine_ref.shape[3])
    modes = jnp.dot(coef_ref[...], rows, preferred_element_type=jnp.float32)
    modes = modes.astype(jnp.bfloat16)
    for f in range(BINS):
        for part in range(2):
            start = (f * 2 + part) * MODES
            out_ref[f, part, 0] = modes[start : start + MODES]


def local(snapshots, space_count):
    points = snapshots.shape[3]
    cut = points // CUTS
    chunks = COMPS * CUTS
    series = jnp.transpose(snapshots, (0, 2, 1, 3)).reshape(COMPS, STEPS, points)
    vmem = pl.BlockSpec(memory_space=pltpu.VMEM)
    mine, coef, energies = pl.pallas_call(
        functools.partial(spectra_kernel, cut, float(COMPS * points * space_count)),
        out_shape=(
            jax.ShapeDtypeStruct((chunks, BLOCKS, ROWS, cut), jnp.bfloat16),
            jax.ShapeDtypeStruct((BINS * 2 * MODES, BLOCKS * ROWS), jnp.bfloat16),
            jax.ShapeDtypeStruct((MODES, BINS), jnp.float32),
        ),
        in_specs=[vmem, pl.BlockSpec(memory_space=pl.ANY)],
        out_specs=(vmem, vmem, vmem),
        scratch_shapes=[
            pltpu.VMEM((2, STEPS, cut), jnp.bfloat16),
            pltpu.VMEM((chunks, BLOCKS, ROWS, cut), jnp.bfloat16),
            pltpu.VMEM((BLOCKS * ROWS, BLOCKS * ROWS), jnp.float32),
            pltpu.VMEM((16, BLOCKS, BLOCKS * ROWS), jnp.float32),
            pltpu.VMEM((2, BLOCKS, BLOCKS, LANES), jnp.float32),
            pltpu.VMEM((2, BINS * 2 * MODES, LANES), jnp.float32),
            pltpu.SemaphoreType.DMA((2,)),
            pltpu.SemaphoreType.DMA((chunks, 16)),
            pltpu.SemaphoreType.DMA((chunks, 16)),
            pltpu.SemaphoreType.DMA((16,)),
            pltpu.SemaphoreType.DMA((16,)),
        ],
        compiler_params=pltpu.CompilerParams(
            collective_id=0, has_side_effects=True, vmem_limit_bytes=VMEM_BYTES
        ),
        cost_estimate=pl.CostEstimate(
            flops=4 * STEPS * STEPS * COMPS * points,
            bytes_accessed=2 * STEPS * COMPS * points,
            transcendentals=0,
        ),
        name="spectra_exchange",
    )(spectral_table(), series)
    modes = pl.pallas_call(
        modes_kernel,
        grid=(chunks,),
        out_shape=jax.ShapeDtypeStruct((BINS, 2, COMPS, MODES, points), jnp.bfloat16),
        in_specs=[vmem, vmem],
        out_specs=pl.BlockSpec(
            (BINS, 2, 1, MODES, cut), lambda k: (0, 0, k // CUTS, 0, lax.rem(k, CUTS))
        ),
        compiler_params=pltpu.CompilerParams(vmem_limit_bytes=VMEM_BYTES),
        cost_estimate=pl.CostEstimate(
            flops=4 * STEPS * BINS * 2 * MODES * COMPS * points,
            bytes_accessed=2 * STEPS * COMPS * points,
            transcendentals=0,
        ),
        name="modes_product",
    )(coef, mine)
    return jnp.transpose(modes, (0, 1, 3, 2, 4)), energies.T


def solution(mesh):
    in_specs = (P("tblock", None, None, "space"),)
    out_specs = (P("tblock", None, None, None, "space"), P("tblock", None))
    body = functools.partial(local, space_count=mesh.shape["space"])
    return jax.shard_map(body, mesh=mesh, in_specs=in_specs, out_specs=out_specs, check_vma=False)
```

time: 399 us -> 260 us (0.65)
  Pallas kernels: 0 us -> 258 us
  waiting for transfers between devices: 222 us -> 0 us
  blocking collectives: 77.2 us -> 0 us
  matrix products: 48.7 us -> 0 us
  local copies, waits for them, and re-layouts: 29 us -> 0.58 us
  other arithmetic: 10.5 us -> 0 us
  starting transfers between devices: 8.59 us -> 0 us
    pallas_call x0 -> x2, Pallas kernels: none -> 258 us  [the longest x1 248 us: local(): pl.pallas_call(functools.partial(spectra_kernel, cut, float(COMPS * point...]
    all_to_all x1 -> x0, waiting for transfers between devices: 222 us -> none  [local(): lax.all_to_all(spectra, 'tblock', split_axis=0, concat_axis=2, tiled=True)]
    psum x1 -> x0, blocking collectives: 77.2 us -> none  [local(): totals = lax.psum(partial_sums, 'space')]
    dot_general x31 -> x0, matrix products: 48.7 us -> none  [the longest x1 18.6 us: local(): jnp.einsum('frbx,fsex->frsbe', mine, mine, preferred_element_type=jnp.flo...]
    reshape x1 -> x0, local copies, waits for them, and re-layouts: 14.2 us -> none  [local(): spectra = spectra.reshape(half_count, 2, 1, width)]
    unnamed x4 -> x3, local copies, waits for them, and re-layouts: 14.4 us -> 0.58 us
    all_to_all x1 -> x0, starting transfers between devices: 8.59 us -> none  [local(): lax.all_to_all(spectra, 'tblock', split_axis=0, concat_axis=2, tiled=True)]
    reduce_sum x43 -> x0, other arithmetic: 8.45 us -> none  [the longest x18 4.22 us: orthonormal(): jnp.sum(base_real * vec_real + base_imag * vec_imag, axis=1, keepdims=True)]
  transfers between devices with their start and end apart: 1 -> 0, of which waited for: 1 -> 0; matrix products, arithmetic and copies ran while one was open for 0% -> 0% of each run, Pallas kernels for 0% -> 0%
where the time goes in v1:
time: 260 us; the launch traced here: 259 us
  Pallas kernels  258 us (99%)
    pallas_call x1, Pallas kernels, local(): pl.pallas_call(functools.partial(spectra_kernel, cut, float(COMPS * point...  248 us
    pallas_call x1, Pallas kernels, local(): pl.pallas_call(modes_kernel, grid=(chunks,), out_shape=jax.ShapeDtypeStru...  10 us

profile of v1, /device:TPU:32, one launch (start us, length us, event | category | flops | bytes accessed | tf_op | source)
XLA Modules:
  0.0 259.2 jit_solution(5716067330416899973)
XLA Ops:
  0.6 247.9 %spectra_exchange.1 = (bf16[12,16,16,1664]{3,2,1,0:T(8,128)(2,1)}, bf16[64,256]{1,0:T(8,128)(2,1)}, f32[4,8]{1,0:T(4,128)}) custom-call(bf16[256,256]{1,0:T(8,128)(2,1)} %constant.4.table_ref, bf16[3,256,6656]{2,1,0:T(8,128)(2,1)} %bitcast.7), custom_call_target="tpu_custom_call" | custom-call | flops 5234491392 | bytes 10223616 | tf_op jit(solution)/shard_map/spectra_exchange/pallas_call | solution.py:322
  248.6 0.0 copy-start
  248.6 10.0 %modes_product.1 = bf16[8,2,3,4,6656]{4,3,2,1,0:T(4,128)(2,1)} custom-call(bf16[64,256]{1,0:T(8,128)(2,1)} %get-tuple-element.5.coef_ref, bf16[12,16,16,1664]{3,2,1,0:T(8,128)(2,1)} %get-tuple-element.6.mine_ref), custom_call_target="tpu_custom_call" | custom-call | flops 1308622848 | bytes 10223616 | tf_op jit(solution)/shard_map/modes_product/pallas_call | solution.py:354
  258.6 0.0 copy-done
  258.6 0.6 copy.5
Async XLA Ops:
  248.6 10.0 %copy-start = (f32[4,8]{1,0:T(4,128)S(1)}, f32[4,8]{1,0:T(4,128)}, u32[]{:S(2)}) copy-start(f32[4,8]{1,0:T(4,128)} %get-tuple-element.7) | copy-start | bytes 388

commit v2 on v1

--- a/solution.py
+++ b/solution.py
@@ -19,7 +19,7 @@
 CUTS = 4
 LANES = 128
 MESH = pl.DeviceIdType.MESH
-VMEM_BYTES = 56 * 2**20
+VMEM_BYTES = 44 * 2**20
 
 
 def spectral_table():
@@ -31,7 +31,7 @@
     window = np.float32(0.5) - np.float32(0.5) * swing
     scaled = window / np.float32(math.sqrt(0.375 * STEPS))
     rows = np.stack([scaled * np.cos(angle), -scaled * np.sin(angle)], axis=1)
-    return jnp.asarray(rows.reshape(STEPS, STEPS).astype(np.float32)).astype(jnp.bfloat16)
+    return jnp.asarray(rows.reshape(STEPS, STEPS).astype(np.float32))
 
 
 def pack_gram(total):
@@ -222,9 +222,8 @@
 
     def make(k):
         take(k).wait()
-        spectra = jnp.dot(
-            table_ref[...], taken_ref[lax.rem(k, 2)], preferred_element_type=jnp.float32
-        )
+        table = table_ref[...].astype(jnp.bfloat16)
+        spectra = jnp.dot(table, taken_ref[lax.rem(k, 2)], preferred_element_type=jnp.float32)
         made_ref[k] = spectra.astype(jnp.bfloat16).reshape(BLOCKS, ROWS, cut)
         mine_ref[k, me] = made_ref[k, me]
 
@@ -302,8 +301,13 @@
         exchange(d, False).wait_send()
 
 
-def modes_kernel(coef_ref, mine_ref, out_ref):
+def modes_kernel(coef_ref, mine_ref, energy_ref, out_ref, energy_out_ref):
     k = pl.program_id(0)
+
+    @pl.when(k == 0)
+    def _():
+        energy_out_ref[...] = energy_ref[...]
+
     rows = mine_ref[k].reshape(BLOCKS * ROWS, mine_ref.shape[3])
     modes = jnp.dot(coef_ref[...], rows, preferred_element_type=jnp.float32)
     modes = modes.astype(jnp.bfloat16)
@@ -322,11 +326,11 @@
     mine, coef, energies = pl.pallas_call(
         functools.partial(spectra_kernel, cut, float(COMPS * points * space_count)),
         out_shape=(
-            jax.ShapeDtypeStruct((chunks, BLOCKS, ROWS, cut), jnp.bfloat16),
+            pltpu.VMEM((chunks, BLOCKS, ROWS, cut), jnp.bfloat16),
             jax.ShapeDtypeStruct((BINS * 2 * MODES, BLOCKS * ROWS), jnp.bfloat16),
             jax.ShapeDtypeStruct((MODES, BINS), jnp.float32),
         ),
-        in_specs=[vmem, pl.BlockSpec(memory_space=pl.ANY)],
+        in_specs=[vmem, pl.BlockSpec(memory_space=pltpu.HBM)],
         out_specs=(vmem, vmem, vmem),
         scratch_shapes=[
             pltpu.VMEM((2, STEPS, cut), jnp.bfloat16),
@@ -351,13 +355,19 @@
         ),
         name="spectra_exchange",
     )(spectral_table(), series)
-    modes = pl.pallas_call(
+    modes, energies = pl.pallas_call(
         modes_kernel,
         grid=(chunks,),
-        out_shape=jax.ShapeDtypeStruct((BINS, 2, COMPS, MODES, points), jnp.bfloat16),
-        in_specs=[vmem, vmem],
-        out_specs=pl.BlockSpec(
-            (BINS, 2, 1, MODES, cut), lambda k: (0, 0, k // CUTS, 0, lax.rem(k, CUTS))
+        out_shape=(
+            jax.ShapeDtypeStruct((BINS, 2, COMPS, MODES, points), jnp.bfloat16),
+            jax.ShapeDtypeStruct((MODES, BINS), jnp.float32),
+        ),
+        in_specs=[vmem, vmem, vmem],
+        out_specs=(
+            pl.BlockSpec(
+                (BINS, 2, 1, MODES, cut), lambda k: (0, 0, k // CUTS, 0, lax.rem(k, CUTS))
+            ),
+            vmem,
         ),
         compiler_params=pltpu.CompilerParams(vmem_limit_bytes=VMEM_BYTES),
         cost_estimate=pl.CostEstimate(
@@ -366,7 +376,7 @@
             transcendentals=0,
         ),
         name="modes_product",
-    )(coef, mine)
+    )(coef, mine, energies)
     return jnp.transpose(modes, (0, 1, 3, 2, 4)), energies.T
 
 

time: 260 us -> 252 us (0.969)
  Pallas kernels: 258 us -> 250 us
    pallas_call x1, Pallas kernels: 10 us -> 6.1 us  [local(): pl.pallas_call(modes_kernel, grid=(chunks,), out_shape=(jax.ShapeDtypeStr...]
    pallas_call x1, Pallas kernels: 248 us -> 244 us  [local(): pl.pallas_call(functools.partial(spectra_kernel, cut, float(COMPS * point...]
where the time goes in v2:
time: 252 us; the launch traced here: 251 us
  Pallas kernels  250 us (99%)
    pallas_call x1, Pallas kernels, local(): pl.pallas_call(functools.partial(spectra_kernel, cut, float(COMPS * point...  244 us
    pallas_call x1, Pallas kernels, local(): pl.pallas_call(modes_kernel, grid=(chunks,), out_shape=(jax.ShapeDtypeStr...  6.1 us

profile of v2, /device:TPU:32, one launch (start us, length us, event | category | flops | bytes accessed | tf_op | source)
XLA Modules:
  0.0 250.8 jit_solution(8373104992546187629)
XLA Ops:
  0.6 244.1 %spectra_exchange.1 = (bf16[12,16,16,1664]{3,2,1,0:T(8,128)(2,1)S(1)}, bf16[64,256]{1,0:T(8,128)(2,1)S(1)}, f32[4,8]{1,0:T(4,128)S(1)}) custom-call(f32[256,256]{1,0:T(8,128)} %constant.2.clone.table_ref, bf16[3,256,6656]{2,1,0:T(8,128)(2,1)} %bitcast.5), custom_call_target="tpu_custom_call" | custom-call | flops 5234491392 | bytes 10223616 | tf_op jit(solution)/shard_map/spectra_exchange/pallas_call | solution.py:326
  244.7 6.1 %modes_product.1 = (bf16[8,2,3,4,6656]{4,3,2,1,0:T(4,128)(2,1)}, f32[4,8]{1,0:T(4,128)}) custom-call(bf16[64,256]{1,0:T(8,128)(2,1)S(1)} %get-tuple-element.7.coef_ref, bf16[12,16,16,1664]{3,2,1,0:T(8,128)(2,1)S(1)} %get-tuple-element.8.mine_ref, f32[4,8]{1,0:T(4,128)S(1)} %get-tuple-element.9.energy_ref), custom_call_target="tpu_custom_call" | custom-call | flops 1308622848 | bytes 10223616 | tf_op jit(solution)/shard_map/modes_product/pallas_call | solution.py:358

commit v3 on v2

--- a/solution.py
+++ b/solution.py
@@ -16,7 +16,7 @@
 BINS = 8
 ROWS = 2 * BINS
 COMPS = 3
-CUTS = 4
+CUTS = 2
 LANES = 128
 MESH = pl.DeviceIdType.MESH
 VMEM_BYTES = 44 * 2**20
@@ -182,14 +182,6 @@
 
     peers = [(dz, dc) for dz in (4, 3, 5, 2, 6, 1, 7, 0) for dc in (0, 1)][:-2] + [(0, 1)]
 
-    barrier = pltpu.get_barrier_semaphore()
-    for dz, dc in peers:
-        pl.semaphore_signal(barrier, inc=1, device_id={"tblock": peer(dz, dc)}, device_id_type=MESH)
-    for d in range(1, 16):
-        pl.semaphore_signal(
-            barrier, inc=1, device_id={"space": lax.rem(here + d, 16)}, device_id_type=MESH
-        )
-
     def take(k):
         comp = k // CUTS
         start = pl.multiple_of(lax.rem(k, CUTS) * cut, LANES)
@@ -229,6 +221,14 @@
 
     take(0).start()
     take(1).start()
+    barrier = pltpu.get_barrier_semaphore()
+    for dz, dc in peers:
+        pl.semaphore_signal(barrier, inc=1, device_id={"tblock": peer(dz, dc)}, device_id_type=MESH)
+    for d in range(1, 16):
+        pl.semaphore_signal(
+            barrier, inc=1, device_id={"space": lax.rem(here + d, 16)}, device_id_type=MESH
+        )
+
     make(0)
     pl.semaphore_wait(barrier, 30)
     for dz, dc in peers:
@@ -301,20 +301,27 @@
         exchange(d, False).wait_send()
 
 
-def modes_kernel(coef_ref, mine_ref, energy_ref, out_ref, energy_out_ref):
-    k = pl.program_id(0)
-
-    @pl.when(k == 0)
-    def _():
-        energy_out_ref[...] = energy_ref[...]
-
-    rows = mine_ref[k].reshape(BLOCKS * ROWS, mine_ref.shape[3])
-    modes = jnp.dot(coef_ref[...], rows, preferred_element_type=jnp.float32)
-    modes = modes.astype(jnp.bfloat16)
-    for f in range(BINS):
-        for part in range(2):
-            start = (f * 2 + part) * MODES
-            out_ref[f, part, 0] = modes[start : start + MODES]
+def modes_kernel(coef_ref, mine_ref, energy_ref, out_ref, energy_out_ref, held_ref, sem):
+    chunks, cut = mine_ref.shape[0], mine_ref.shape[3]
+
+    def put(k):
+        columns = pl.ds(k % CUTS * cut, cut)
+        return pltpu.make_async_copy(
+            held_ref.at[k], out_ref.at[:, :, k // CUTS, :, columns], sem.at[k]
+        )
+
+    for k in range(chunks):
+        rows = mine_ref[k].reshape(BLOCKS * ROWS, cut)
+        modes = jnp.dot(coef_ref[...], rows, preferred_element_type=jnp.float32)
+        modes = modes.astype(jnp.bfloat16)
+        for f in range(BINS):
+            for part in range(2):
+                start = (f * 2 + part) * MODES
+                held_ref[k, f, part] = modes[start : start + MODES]
+        put(k).start()
+    energy_out_ref[...] = energy_ref[...]
+    for k in range(chunks):
+        put(k).wait()
 
 
 def local(snapshots, space_count):
@@ -357,18 +364,16 @@
     )(spectral_table(), series)
     modes, energies = pl.pallas_call(
         modes_kernel,
-        grid=(chunks,),
         out_shape=(
             jax.ShapeDtypeStruct((BINS, 2, COMPS, MODES, points), jnp.bfloat16),
             jax.ShapeDtypeStruct((MODES, BINS), jnp.float32),
         ),
         in_specs=[vmem, vmem, vmem],
-        out_specs=(
-            pl.BlockSpec(
-                (BINS, 2, 1, MODES, cut), lambda k: (0, 0, k // CUTS, 0, lax.rem(k, CUTS))
-            ),
-            vmem,
-        ),
+        out_specs=(pl.BlockSpec(memory_space=pltpu.HBM), vmem),
+        scratch_shapes=[
+            pltpu.VMEM((chunks, BINS, 2, MODES, cut), jnp.bfloat16),
+            pltpu.SemaphoreType.DMA((chunks,)),
+        ],
         compiler_params=pltpu.CompilerParams(vmem_limit_bytes=VMEM_BYTES),
         cost_estimate=pl.CostEstimate(
             flops=4 * STEPS * BINS * 2 * MODES * COMPS * points,

time: 252 us -> 247 us (0.980)
  Pallas kernels: 250 us -> 245 us
    pallas_call x1, Pallas kernels: 6.1 us -> 3.28 us  [local(): pl.pallas_call(modes_kernel, out_shape=(jax.ShapeDtypeStruct((BINS, 2, CO...]
where the time goes in v3:
time: 247 us; the launch traced here: 246 us
  Pallas kernels  245 us (99%)
    pallas_call x1, Pallas kernels, local(): pl.pallas_call(functools.partial(spectra_kernel, cut, float(COMPS * point...  242 us

profile of v3, /device:TPU:32, one launch (start us, length us, event | category | flops | bytes accessed | tf_op | source)
XLA Modules:
  0.0 246.1 jit_solution(7933083656428080537)
XLA Ops:
  0.6 242.1 %spectra_exchange.1 = (bf16[6,16,16,3328]{3,2,1,0:T(8,128)(2,1)S(1)}, bf16[64,256]{1,0:T(8,128)(2,1)S(1)}, f32[4,8]{1,0:T(4,128)S(1)}) custom-call(f32[256,256]{1,0:T(8,128)} %constant.2.clone.table_ref, bf16[3,256,6656]{2,1,0:T(8,128)(2,1)} %bitcast.5), custom_call_target="tpu_custom_call" | custom-call | flops 5234491392 | bytes 10223616 | tf_op jit(solution)/shard_map/spectra_exchange/pallas_call | solution.py:333
  242.8 3.3 %modes_product.1 = (bf16[8,2,3,4,6656]{4,3,2,1,0:T(4,128)(2,1)}, f32[4,8]{1,0:T(4,128)}) custom-call(bf16[64,256]{1,0:T(8,128)(2,1)S(1)} %get-tuple-element.7.coef_ref, bf16[6,16,16,3328]{3,2,1,0:T(8,128)(2,1)S(1)} %get-tuple-element.8.mine_ref, f32[4,8]{1,0:T(4,128)S(1)} %get-tuple-element.9.energy_ref), custom_call_target="tpu_custom_call" | custom-call | flops 1308622848 | bytes 10223616 | tf_op jit(solution)/shard_map/modes_product/pallas_call | solution.py:365

commit v4 on v3

--- a/solution.py
+++ b/solution.py
@@ -17,6 +17,8 @@
 ROWS = 2 * BINS
 COMPS = 3
 CUTS = 2
+LEVELS = 8
+SIDE = 4
 LANES = 128
 MESH = pl.DeviceIdType.MESH
 VMEM_BYTES = 44 * 2**20
@@ -32,6 +34,11 @@
     scaled = window / np.float32(math.sqrt(0.375 * STEPS))
     rows = np.stack([scaled * np.cos(angle), -scaled * np.sin(angle)], axis=1)
     return jnp.asarray(rows.reshape(STEPS, STEPS).astype(np.float32))
+
+
+def chunk_widths(points):
+    first, last = 4 * LANES, 8 * LANES
+    return ((first, points - first), (points,), (points - last, last))
 
 
 def pack_gram(total):
@@ -152,49 +159,76 @@
 
 
 def spectra_kernel(
-    cut,
+    points,
     scale,
     table_ref,
     series_ref,
     mine_ref,
     coef_ref,
     energy_ref,
+    rows_ref,
+    round_ref,
     taken_ref,
     made_ref,
     total_ref,
     packed_ref,
     gram_ref,
     order_ref,
+    table_sem,
     take_sem,
     send_sem,
     recv_sem,
     sum_send_sem,
     sum_recv_sem,
+    ring_sem,
+    plane_sem,
 ):
-    chunks = COMPS * CUTS
+    chunks = []
+    for comp, widths in enumerate(chunk_widths(points)):
+        start = 0
+        for width in widths:
+            chunks.append((comp, start, width))
+            start += width
     here = lax.axis_index("space")
     me = lax.axis_index("tblock")
     level = me // 2
     core = lax.rem(me, 2)
+    high = here // SIDE
+    wide = lax.rem(here, SIDE)
 
     def peer(dz, dc):
-        return lax.rem(level + dz, 8) * 2 + lax.rem(core + dc, 2)
-
-    peers = [(dz, dc) for dz in (4, 3, 5, 2, 6, 1, 7, 0) for dc in (0, 1)][:-2] + [(0, 1)]
+        return lax.rem(level + dz, LEVELS) * 2 + lax.rem(core + dc, 2)
+
+    def plane(dy, dx):
+        return lax.rem(high + dy, SIDE) * SIDE + lax.rem(wide + dx, SIDE)
+
+    def signal(sem, **device):
+        pl.semaphore_signal(sem, inc=1, device_id=device, device_id_type=MESH)
+
+    rings = [[(0, 1)]] + [
+        [(dz, dc) for dz in sorted({far, LEVELS - far}) for dc in (0, 1)]
+        for far in range(1, LEVELS // 2 + 1)
+    ]
+    rings = [rings[1] + rings[0]] + rings[2:]
+    peers = [pair for ring in rings[::-1] for pair in ring]
 
     def take(k):
-        comp = k // CUTS
-        start = pl.multiple_of(lax.rem(k, CUTS) * cut, LANES)
-        slot = lax.rem(k, 2)
+        comp, start, width = chunks[k]
         return pltpu.make_async_copy(
-            series_ref.at[comp, :, pl.ds(start, cut)], taken_ref.at[slot], take_sem.at[slot]
-        )
+            series_ref.at[comp, :, pl.ds(start, width)],
+            taken_ref.at[k % 2, :, pl.ds(0, width)],
+            take_sem.at[k % 2],
+        )
+
+    def columns(k):
+        comp, start, width = chunks[k]
+        return pl.ds(comp * points + start, width)
 
     def send(k, dz, dc):
         to = peer(dz, dc)
         return pltpu.make_async_remote_copy(
-            src_ref=made_ref.at[k, to],
-            dst_ref=mine_ref.at[k, me],
+            src_ref=made_ref.at[to, :, columns(k)],
+            dst_ref=mine_ref.at[me, :, columns(k)],
             send_sem=send_sem.at[k, to],
             recv_sem=recv_sem.at[k, me],
             device_id={"tblock": to},
@@ -204,8 +238,8 @@
     def arrival(k, dz, dc):
         sender = peer(dz, dc)
         return pltpu.make_async_remote_copy(
-            src_ref=made_ref.at[k, sender],
-            dst_ref=mine_ref.at[k, sender],
+            src_ref=made_ref.at[sender, :, columns(k)],
+            dst_ref=mine_ref.at[sender, :, columns(k)],
             send_sem=send_sem.at[k, sender],
             recv_sem=recv_sem.at[k, sender],
             device_id={"tblock": sender},
@@ -213,56 +247,72 @@
         )
 
     def make(k):
+        width = chunks[k][2]
         take(k).wait()
-        table = table_ref[...].astype(jnp.bfloat16)
-        spectra = jnp.dot(table, taken_ref[lax.rem(k, 2)], preferred_element_type=jnp.float32)
-        made_ref[k] = spectra.astype(jnp.bfloat16).reshape(BLOCKS, ROWS, cut)
-        mine_ref[k, me] = made_ref[k, me]
-
+        spectra = jnp.dot(
+            round_ref[...], taken_ref[k % 2, :, :width], preferred_element_type=jnp.float32
+        )
+        made_ref[:, :, columns(k)] = spectra.astype(jnp.bfloat16).reshape(BLOCKS, ROWS, width)
+        if k + 2 < len(chunks):
+            take(k + 2).start()
+        mine_ref[me, :, columns(k)] = made_ref[me, :, columns(k)]
+
+    table = pltpu.make_async_copy(table_ref, rows_ref, table_sem)
+    table.start()
     take(0).start()
+    barrier = pltpu.get_barrier_semaphore()
+    for dz, dc in rings[0]:
+        signal(barrier, tblock=peer(dz, dc))
+    sides = [(0, 1), (0, SIDE - 1), (1, 0), (SIDE - 1, 0)]
+    for dy, dx in sides:
+        signal(barrier, space=plane(dy, dx))
     take(1).start()
-    barrier = pltpu.get_barrier_semaphore()
-    for dz, dc in peers:
-        pl.semaphore_signal(barrier, inc=1, device_id={"tblock": peer(dz, dc)}, device_id_type=MESH)
-    for d in range(1, 16):
-        pl.semaphore_signal(
-            barrier, inc=1, device_id={"space": lax.rem(here + d, 16)}, device_id_type=MESH
-        )
-
+    table.wait()
+    round_ref[...] = rows_ref[...].astype(jnp.bfloat16)
     make(0)
-    pl.semaphore_wait(barrier, 30)
-    for dz, dc in peers:
-        send(0, dz, dc).start()
-
-    def make_and_send(k, carry):
-        @pl.when(k + 1 < chunks)
-        def _():
-            take(k + 1).start()
-
+    pl.semaphore_wait(barrier, len(rings[0]) + len(sides))
+
+    for r, ring in enumerate(rings):
+        if r:
+            pl.semaphore_wait(ring_sem.at[r - 1, 0], 1)
+            pl.semaphore_wait(ring_sem.at[r - 1, 1], 1)
+        if r + 1 < len(rings):
+            signal(ring_sem.at[r, 0], tblock=peer(1, 0))
+            signal(ring_sem.at[r, 1], tblock=peer(LEVELS - 1, 0))
+        for dz, dc in ring:
+            send(0, dz, dc).start()
+        if r == 0:
+            signal(plane_sem.at[0], space=plane(0, SIDE - 1))
+    for k in range(1, len(chunks)):
         make(k)
         for dz, dc in peers:
             send(k, dz, dc).start()
-        return carry
-
-    lax.fori_loop(1, chunks, make_and_send, 0)
-
-    total_ref[...] = jnp.zeros_like(total_ref)
-
-    def gather(k, carry):
+        if k == 1:
+            pl.semaphore_wait(plane_sem.at[0], 1)
+            signal(plane_sem.at[1], space=plane(1, 0))
+            signal(plane_sem.at[2], space=plane(SIDE - 1, 0))
+        if k == 2:
+            pl.semaphore_wait(plane_sem.at[1], 1)
+            pl.semaphore_wait(plane_sem.at[2], 1)
+            signal(plane_sem.at[3], space=plane(SIDE - 1, 0))
+    pl.semaphore_wait(plane_sem.at[3], 1)
+
+    for k in range(len(chunks)):
         for dz, dc in peers:
             arrival(k, dz, dc).wait_recv()
-        rows = mine_ref[k].reshape(BLOCKS * ROWS, cut)
-        total_ref[...] += lax.dot_general(
+        rows = mine_ref[:, :, columns(k)].reshape(BLOCKS * ROWS, chunks[k][2])
+        part = lax.dot_general(
             rows, rows, (((1,), (1,)), ((), ())), preferred_element_type=jnp.float32
         )
-        return carry
-
-    lax.fori_loop(0, chunks, gather, 0)
+        if k == 0:
+            total_ref[...] = part
+        else:
+            total_ref[...] += part
 
     packed_ref[here] = pack_gram(total_ref[...])
 
     def exchange(d, arriving):
-        other = lax.rem(here + d, 16)
+        other = lax.rem(here + d, SIDE * SIDE)
         slot = other if arriving else here
         return pltpu.make_async_remote_copy(
             src_ref=packed_ref.at[here],
@@ -273,36 +323,34 @@
             device_id_type=MESH,
         )
 
-    for d in range(1, 16):
+    others = range(1, SIDE * SIDE)
+    for d in others:
         exchange(d, False).start()
-    for d in range(1, 16):
+    for d in others:
         exchange(d, True).wait_recv()
     packed = packed_ref[0]
-    for s in range(1, 16):
+    for s in others:
         packed = packed + packed_ref[s]
     packed = packed / scale
 
     vec_real, vec_imag, energies = leading_modes(packed, gram_ref)
     coef_ref[...] = coefficient_matrix(vec_real, vec_imag, energies, order_ref)
-    wide = jnp.concatenate(energies, axis=0)
+    spread = jnp.concatenate(energies, axis=0)
     lane = lax.broadcasted_iota(jnp.int32, (MODES, LANES), 1)
-    narrow = wide
+    narrow = spread
     for f in range(1, BINS):
-        narrow = jnp.where(lane == f, pltpu.roll(wide, LANES - f, 1), narrow)
+        narrow = jnp.where(lane == f, pltpu.roll(spread, LANES - f, 1), narrow)
     energy_ref[...] = narrow[:, :BINS]
 
-    def finish(k, carry):
+    for k in range(len(chunks)):
         for dz, dc in peers:
             send(k, dz, dc).wait_send()
-        return carry
-
-    lax.fori_loop(0, chunks, finish, 0)
-    for d in range(1, 16):
+    for d in others:
         exchange(d, False).wait_send()
 
 
 def modes_kernel(coef_ref, mine_ref, energy_ref, out_ref, energy_out_ref, held_ref, sem):
-    chunks, cut = mine_ref.shape[0], mine_ref.shape[3]
+    chunks, cut = held_ref.shape[0], held_ref.shape[4]
 
     def put(k):
         columns = pl.ds(k % CUTS * cut, cut)
@@ -311,7 +359,7 @@
         )
 
     for k in range(chunks):
-        rows = mine_ref[k].reshape(BLOCKS * ROWS, cut)
+        rows = mine_ref[:, :, k * cut : (k + 1) * cut].reshape(BLOCKS * ROWS, cut)
         modes = jnp.dot(coef_ref[...], rows, preferred_element_type=jnp.float32)
         modes = modes.astype(jnp.bfloat16)
         for f in range(BINS):
@@ -327,30 +375,37 @@
 def local(snapshots, space_count):
     points = snapshots.shape[3]
     cut = points // CUTS
-    chunks = COMPS * CUTS
+    width = COMPS * points
+    pieces = len([w for widths in chunk_widths(points) for w in widths])
     series = jnp.transpose(snapshots, (0, 2, 1, 3)).reshape(COMPS, STEPS, points)
     vmem = pl.BlockSpec(memory_space=pltpu.VMEM)
+    hbm = pl.BlockSpec(memory_space=pltpu.HBM)
     mine, coef, energies = pl.pallas_call(
-        functools.partial(spectra_kernel, cut, float(COMPS * points * space_count)),
+        functools.partial(spectra_kernel, points, float(width * space_count)),
         out_shape=(
-            pltpu.VMEM((chunks, BLOCKS, ROWS, cut), jnp.bfloat16),
+            pltpu.VMEM((BLOCKS, ROWS, width), jnp.bfloat16),
             jax.ShapeDtypeStruct((BINS * 2 * MODES, BLOCKS * ROWS), jnp.bfloat16),
             jax.ShapeDtypeStruct((MODES, BINS), jnp.float32),
         ),
-        in_specs=[vmem, pl.BlockSpec(memory_space=pltpu.HBM)],
+        in_specs=[hbm, hbm],
         out_specs=(vmem, vmem, vmem),
         scratch_shapes=[
-            pltpu.VMEM((2, STEPS, cut), jnp.bfloat16),
-            pltpu.VMEM((chunks, BLOCKS, ROWS, cut), jnp.bfloat16),
+            pltpu.VMEM((STEPS, STEPS), jnp.float32),
+            pltpu.VMEM((STEPS, STEPS), jnp.bfloat16),
+            pltpu.VMEM((2, STEPS, points), jnp.bfloat16),
+            pltpu.VMEM((BLOCKS, ROWS, width), jnp.bfloat16),
             pltpu.VMEM((BLOCKS * ROWS, BLOCKS * ROWS), jnp.float32),
-            pltpu.VMEM((16, BLOCKS, BLOCKS * ROWS), jnp.float32),
+            pltpu.VMEM((SIDE * SIDE, BLOCKS, BLOCKS * ROWS), jnp.float32),
             pltpu.VMEM((2, BLOCKS, BLOCKS, LANES), jnp.float32),
             pltpu.VMEM((2, BINS * 2 * MODES, LANES), jnp.float32),
+            pltpu.SemaphoreType.DMA,
             pltpu.SemaphoreType.DMA((2,)),
-            pltpu.SemaphoreType.DMA((chunks, 16)),
-            pltpu.SemaphoreType.DMA((chunks, 16)),
-            pltpu.SemaphoreType.DMA((16,)),
-            pltpu.SemaphoreType.DMA((16,)),
+            pltpu.SemaphoreType.DMA((pieces, BLOCKS)),
+            pltpu.SemaphoreType.DMA((pieces, BLOCKS)),
+            pltpu.SemaphoreType.DMA((SIDE * SIDE,)),
+            pltpu.SemaphoreType.DMA((SIDE * SIDE,)),
+            pltpu.SemaphoreType.REGULAR((LEVELS // 2 - 1, 2)),
+            pltpu.SemaphoreType.REGULAR((4,)),
         ],
         compiler_params=pltpu.CompilerParams(
             collective_id=0, has_side_effects=True, vmem_limit_bytes=VMEM_BYTES
@@ -369,10 +424,10 @@
             jax.ShapeDtypeStruct((MODES, BINS), jnp.float32),
         ),
         in_specs=[vmem, vmem, vmem],
-        out_specs=(pl.BlockSpec(memory_space=pltpu.HBM), vmem),
+        out_specs=(hbm, vmem),
         scratch_shapes=[
-            pltpu.VMEM((chunks, BINS, 2, MODES, cut), jnp.bfloat16),
-            pltpu.SemaphoreType.DMA((chunks,)),
+            pltpu.VMEM((COMPS * CUTS, BINS, 2, MODES, cut), jnp.bfloat16),
+            pltpu.SemaphoreType.DMA((COMPS * CUTS,)),
         ],
         compiler_params=pltpu.CompilerParams(vmem_limit_bytes=VMEM_BYTES),
         cost_estimate=pl.CostEstimate(

time: 247 us -> 245 us (level)
  no operation moved by 1% of the time
where the time goes in v4:
time: 245 us; the launch traced here: 244 us
  Pallas kernels  243 us (99%)
    pallas_call x1, Pallas kernels, local(): pl.pallas_call(functools.partial(spectra_kernel, points, float(width * sp...  240 us

profile of v4, /device:TPU:32, one launch (start us, length us, event | category | flops | bytes accessed | tf_op | source)
XLA Modules:
  0.0 243.9 jit_solution(11577036244969745975)
XLA Ops:
  0.6 240.0 %spectra_exchange.1 = (bf16[16,16,19968]{2,1,0:T(8,128)(2,1)S(1)}, bf16[64,256]{1,0:T(8,128)(2,1)S(1)}, f32[4,8]{1,0:T(4,128)S(1)}) custom-call(f32[256,256]{1,0:T(8,128)} %constant.2.clone.table_ref, bf16[3,256,6656]{2,1,0:T(8,128)(2,1)} %bitcast.5), custom_call_target="tpu_custom_call" | custom-call | flops 5234491392 | bytes 10223616 | tf_op jit(solution)/shard_map/spectra_exchange/pallas_call | solution.py:383
  240.6 3.3 %modes_product.1 = (bf16[8,2,3,4,6656]{4,3,2,1,0:T(4,128)(2,1)}, f32[4,8]{1,0:T(4,128)}) custom-call(bf16[64,256]{1,0:T(8,128)(2,1)S(1)} %get-tuple-element.7.coef_ref, bf16[16,16,19968]{2,1,0:T(8,128)(2,1)S(1)} %get-tuple-element.8.mine_ref, f32[4,8]{1,0:T(4,128)S(1)} %get-tuple-element.9.energy_ref), custom_call_target="tpu_custom_call" | custom-call | flops 1308622848 | bytes 10223616 | tf_op jit(solution)/shard_map/modes_product/pallas_call | solution.py:420

commit v5 on v4

--- a/solution.py
+++ b/solution.py
@@ -16,12 +16,15 @@
 BINS = 8
 ROWS = 2 * BINS
 COMPS = 3
-CUTS = 2
+GROUPS = 2
+GROUP_BINS = BINS // GROUPS
+GROUP_ROWS = ROWS // GROUPS
 LEVELS = 8
 SIDE = 4
 LANES = 128
 MESH = pl.DeviceIdType.MESH
-VMEM_BYTES = 44 * 2**20
+VMEM_BYTES = 50 * 2**20
+MODES_VMEM_BYTES = 16 * 2**20
 
 
 def spectral_table():
@@ -33,12 +36,18 @@
     window = np.float32(0.5) - np.float32(0.5) * swing
     scaled = window / np.float32(math.sqrt(0.375 * STEPS))
     rows = np.stack([scaled * np.cos(angle), -scaled * np.sin(angle)], axis=1)
+    rows = rows.reshape(BLOCKS, GROUPS, GROUP_ROWS, STEPS).transpose(1, 0, 2, 3)
     return jnp.asarray(rows.reshape(STEPS, STEPS).astype(np.float32))
 
 
-def chunk_widths(points):
-    first, last = 4 * LANES, 8 * LANES
-    return ((first, points - first), (points,), (points - last, last))
+def chunk_plan(points):
+    half = points // GROUPS
+    first, second, last = 2 * LANES, 8 * LANES, 8 * LANES
+    made = [(0, 0, first), (0, first, second - first), (0, second, half - second)]
+    sent = [(0, start, width) for _, start, width in made] + [(0, half, (COMPS - 1) * half)]
+    made += [(c, 0, half) for c in range(1, COMPS)]
+    sent += [(1, 0, COMPS * half - last), (1, COMPS * half - last, last)]
+    return made, sent
 
 
 def pack_gram(total):
@@ -56,7 +65,15 @@
     even = lax.broadcasted_iota(jnp.int32, (BLOCKS, width), 1) % 2 == 0
     real = real + pltpu.roll(real, width - 1, 1)
     imag = imag + pltpu.roll(imag, 1, 1)
-    return jnp.where(even, real, imag)
+    both = jnp.where(even, real, imag)
+    left, right = both[:, :LANES], both[:, LANES:]
+    left = left + pltpu.roll(left, LANES - GROUP_ROWS, 1)
+    right = right + pltpu.roll(right, GROUP_ROWS, 1)
+    return jnp.where(first_half((BLOCKS, LANES)), left, right)
+
+
+def first_half(shape):
+    return lax.broadcasted_iota(jnp.int32, shape, 1) % ROWS < GROUP_ROWS
 
 
 def column_sum(value):
@@ -65,9 +82,13 @@
 
 def leading_modes(packed, gram_ref):
     even = lax.broadcasted_iota(jnp.int32, (BLOCKS, LANES), 1) % 2 == 0
+    low = first_half((BLOCKS, LANES))
     per_half = LANES // ROWS
     for half in range(2):
-        part = packed[:, half * LANES : (half + 1) * LANES]
+        if half:
+            part = jnp.where(low, pltpu.roll(packed, LANES - GROUP_ROWS, 1), packed)
+        else:
+            part = jnp.where(low, packed, pltpu.roll(packed, GROUP_ROWS, 1))
         real = jnp.where(even, part, pltpu.roll(part, 1, 1))
         imag = jnp.where(even, pltpu.roll(part, LANES - 1, 1), part)
         for near in range(per_half):
@@ -158,18 +179,31 @@
     return jnp.concatenate([order_ref[0], order_ref[1]], axis=1).astype(jnp.bfloat16)
 
 
+def group_modes(coef, mine_ref, columns, put):
+    rows = mine_ref[:, :, columns]
+    rows = rows.reshape(BLOCKS * ROWS, rows.shape[2])
+    modes = jnp.dot(coef, rows, preferred_element_type=jnp.float32).astype(jnp.bfloat16)
+    for half in range(GROUPS):
+        for f in range(GROUP_BINS):
+            for part in range(2):
+                start = ((half * GROUP_BINS + f) * 2 + part) * MODES
+                put(f, part, half, modes[start : start + MODES])
+
+
 def spectra_kernel(
     points,
     scale,
     table_ref,
     series_ref,
     mine_ref,
+    done_ref,
     coef_ref,
     energy_ref,
     rows_ref,
     round_ref,
     taken_ref,
     made_ref,
+    early_ref,
     total_ref,
     packed_ref,
     gram_ref,
@@ -183,12 +217,9 @@
     ring_sem,
     plane_sem,
 ):
-    chunks = []
-    for comp, widths in enumerate(chunk_widths(points)):
-        start = 0
-        for width in widths:
-            chunks.append((comp, start, width))
-            start += width
+    half_points = points // GROUPS
+    made, sent = chunk_plan(points)
+    lands = (early_ref, mine_ref)
     here = lax.axis_index("space")
     me = lax.axis_index("tblock")
     level = me // 2
@@ -212,23 +243,20 @@
     rings = [rings[1] + rings[0]] + rings[2:]
     peers = [pair for ring in rings[::-1] for pair in ring]
 
-    def take(k):
-        comp, start, width = chunks[k]
+    def take(k, half):
+        comp, start, width = made[k]
         return pltpu.make_async_copy(
-            series_ref.at[comp, :, pl.ds(start, width)],
-            taken_ref.at[k % 2, :, pl.ds(0, width)],
-            take_sem.at[k % 2],
+            series_ref.at[comp, :, pl.ds(half * half_points + start, width)],
+            taken_ref.at[k % 2, half, :, pl.ds(0, width)],
+            take_sem.at[k % 2, half],
         )
 
-    def columns(k):
-        comp, start, width = chunks[k]
-        return pl.ds(comp * points + start, width)
-
     def send(k, dz, dc):
+        group, start, width = sent[k]
         to = peer(dz, dc)
         return pltpu.make_async_remote_copy(
-            src_ref=made_ref.at[to, :, columns(k)],
-            dst_ref=mine_ref.at[me, :, columns(k)],
+            src_ref=made_ref.at[group, to, :, pl.ds(start, width)],
+            dst_ref=lands[group].at[me, :, pl.ds(start, width)],
             send_sem=send_sem.at[k, to],
             recv_sem=recv_sem.at[k, me],
             device_id={"tblock": to},
@@ -236,10 +264,11 @@
         )
 
     def arrival(k, dz, dc):
+        group, start, width = sent[k]
         sender = peer(dz, dc)
         return pltpu.make_async_remote_copy(
-            src_ref=made_ref.at[sender, :, columns(k)],
-            dst_ref=mine_ref.at[sender, :, columns(k)],
+            src_ref=made_ref.at[group, sender, :, pl.ds(start, width)],
+            dst_ref=lands[group].at[sender, :, pl.ds(start, width)],
             send_sem=send_sem.at[k, sender],
             recv_sem=recv_sem.at[k, sender],
             device_id={"tblock": sender},
@@ -247,26 +276,33 @@
         )
 
     def make(k):
-        width = chunks[k][2]
-        take(k).wait()
-        spectra = jnp.dot(
-            round_ref[...], taken_ref[k % 2, :, :width], preferred_element_type=jnp.float32
-        )
-        made_ref[:, :, columns(k)] = spectra.astype(jnp.bfloat16).reshape(BLOCKS, ROWS, width)
-        if k + 2 < len(chunks):
-            take(k + 2).start()
-        mine_ref[me, :, columns(k)] = made_ref[me, :, columns(k)]
+        comp, start, width = made[k]
+        columns = pl.ds(comp * half_points + start, width)
+        for half in range(GROUPS):
+            take(k, half).wait()
+            spectra = jnp.dot(
+                round_ref[...], taken_ref[k % 2, half, :, :width], preferred_element_type=jnp.float32
+            )
+            made_ref[:, :, pl.ds(half * GROUP_ROWS, GROUP_ROWS), columns] = spectra.astype(
+                jnp.bfloat16
+            ).reshape(GROUPS, BLOCKS, GROUP_ROWS, width)
+            if k + 2 < len(made):
+                take(k + 2, half).start()
+        for group in range(GROUPS):
+            lands[group][me, :, columns] = made_ref[group, me, :, columns]
 
     table = pltpu.make_async_copy(table_ref, rows_ref, table_sem)
     table.start()
-    take(0).start()
+    for half in range(GROUPS):
+        take(0, half).start()
     barrier = pltpu.get_barrier_semaphore()
     for dz, dc in rings[0]:
         signal(barrier, tblock=peer(dz, dc))
     sides = [(0, 1), (0, SIDE - 1), (1, 0), (SIDE - 1, 0)]
     for dy, dx in sides:
         signal(barrier, space=plane(dy, dx))
-    take(1).start()
+    for half in range(GROUPS):
+        take(1, half).start()
     table.wait()
     round_ref[...] = rows_ref[...].astype(jnp.bfloat16)
     make(0)
@@ -283,127 +319,157 @@
             send(0, dz, dc).start()
         if r == 0:
             signal(plane_sem.at[0], space=plane(0, SIDE - 1))
-    for k in range(1, len(chunks)):
+            make(1)
+    for dz, dc in peers:
+        send(1, dz, dc).start()
+    make(2)
+    for dz, dc in peers:
+        send(2, dz, dc).start()
+    pl.semaphore_wait(plane_sem.at[0], 1)
+    signal(plane_sem.at[1], space=plane(1, 0))
+    signal(plane_sem.at[2], space=plane(SIDE - 1, 0))
+    for k in range(3, len(made)):
         make(k)
+    for k in range(3, len(sent)):
         for dz, dc in peers:
             send(k, dz, dc).start()
-        if k == 1:
-            pl.semaphore_wait(plane_sem.at[0], 1)
-            signal(plane_sem.at[1], space=plane(1, 0))
-            signal(plane_sem.at[2], space=plane(SIDE - 1, 0))
-        if k == 2:
-            pl.semaphore_wait(plane_sem.at[1], 1)
-            pl.semaphore_wait(plane_sem.at[2], 1)
-            signal(plane_sem.at[3], space=plane(SIDE - 1, 0))
+    pl.semaphore_wait(plane_sem.at[1], 1)
+    pl.semaphore_wait(plane_sem.at[2], 1)
+    signal(plane_sem.at[3], space=plane(SIDE - 1, 0))
     pl.semaphore_wait(plane_sem.at[3], 1)
 
-    for k in range(len(chunks)):
-        for dz, dc in peers:
-            arrival(k, dz, dc).wait_recv()
-        rows = mine_ref[:, :, columns(k)].reshape(BLOCKS * ROWS, chunks[k][2])
-        part = lax.dot_general(
-            rows, rows, (((1,), (1,)), ((), ())), preferred_element_type=jnp.float32
-        )
-        if k == 0:
-            total_ref[...] = part
-        else:
-            total_ref[...] += part
-
-    packed_ref[here] = pack_gram(total_ref[...])
-
-    def exchange(d, arriving):
+    others = range(1, SIDE * SIDE)
+
+    def exchange(group, d, arriving):
         other = lax.rem(here + d, SIDE * SIDE)
         slot = other if arriving else here
         return pltpu.make_async_remote_copy(
-            src_ref=packed_ref.at[here],
-            dst_ref=packed_ref.at[slot],
-            send_sem=sum_send_sem.at[other],
-            recv_sem=sum_recv_sem.at[slot],
+            src_ref=packed_ref.at[group, here],
+            dst_ref=packed_ref.at[group, slot],
+            send_sem=sum_send_sem.at[group, other],
+            recv_sem=sum_recv_sem.at[group, slot],
             device_id={"space": other},
             device_id_type=MESH,
         )
 
-    others = range(1, SIDE * SIDE)
-    for d in others:
-        exchange(d, False).start()
-    for d in others:
-        exchange(d, True).wait_recv()
-    packed = packed_ref[0]
-    for s in others:
-        packed = packed + packed_ref[s]
-    packed = packed / scale
-
-    vec_real, vec_imag, energies = leading_modes(packed, gram_ref)
-    coef_ref[...] = coefficient_matrix(vec_real, vec_imag, energies, order_ref)
-    spread = jnp.concatenate(energies, axis=0)
+    def solve(group):
+        opened = False
+        for k in range(len(sent)):
+            owner, start, width = sent[k]
+            if owner != group:
+                continue
+            for dz, dc in peers:
+                arrival(k, dz, dc).wait_recv()
+            rows = lands[group][:, :, pl.ds(start, width)].reshape(BLOCKS * ROWS, width)
+            part = lax.dot_general(
+                rows, rows, (((1,), (1,)), ((), ())), preferred_element_type=jnp.float32
+            )
+            total_ref[...] = total_ref[...] + part if opened else part
+            opened = True
+        packed_ref[group, here] = pack_gram(total_ref[...])
+        for d in others:
+            exchange(group, d, False).start()
+        for d in others:
+            exchange(group, d, True).wait_recv()
+        packed = packed_ref[group, 0]
+        for s in others:
+            packed = packed + packed_ref[group, s]
+        vec_real, vec_imag, energies = leading_modes(packed / scale, gram_ref)
+        coef = coefficient_matrix(vec_real, vec_imag, energies, order_ref)
+        return coef, jnp.concatenate(energies, axis=0)
+
     lane = lax.broadcasted_iota(jnp.int32, (MODES, LANES), 1)
-    narrow = spread
-    for f in range(1, BINS):
-        narrow = jnp.where(lane == f, pltpu.roll(spread, LANES - f, 1), narrow)
-    energy_ref[...] = narrow[:, :BINS]
-
-    for k in range(len(chunks)):
+
+    def settle(group, spread):
+        narrow = spread
+        for f in range(GROUP_BINS):
+            to = group * GROUP_BINS + f
+            if to != 2 * f:
+                narrow = jnp.where(lane == to, pltpu.roll(spread, (to - 2 * f) % LANES, 1), narrow)
+        columns = slice(group * GROUP_BINS, (group + 1) * GROUP_BINS)
+        energy_ref[:, columns] = narrow[:, columns]
+
+    coef, spread = solve(0)
+    settle(0, spread)
+    for comp in range(COMPS):
+
+        def put(f, part, half, rows):
+            done_ref[f, part, comp, :, pl.ds(half * half_points, half_points)] = rows
+
+        group_modes(coef, early_ref, pl.ds(comp * half_points, half_points), put)
+
+    coef, spread = solve(1)
+    coef_ref[...] = coef
+    settle(1, spread)
+
+    for k in range(len(sent)):
         for dz, dc in peers:
             send(k, dz, dc).wait_send()
-    for d in others:
-        exchange(d, False).wait_send()
-
-
-def modes_kernel(coef_ref, mine_ref, energy_ref, out_ref, energy_out_ref, held_ref, sem):
-    chunks, cut = held_ref.shape[0], held_ref.shape[4]
-
-    def put(k):
-        columns = pl.ds(k % CUTS * cut, cut)
+    for group in range(GROUPS):
+        for d in others:
+            exchange(group, d, False).wait_send()
+
+
+def modes_kernel(
+    coef_ref, mine_ref, done_ref, energy_ref, out_ref, energy_out_ref, held_ref, sem, done_sem
+):
+    half_points = held_ref.shape[4] // GROUPS
+    early = pltpu.make_async_copy(done_ref, out_ref.at[pl.ds(0, GROUP_BINS)], done_sem.at[0])
+    early.start()
+    energy = pltpu.make_async_copy(energy_ref, energy_out_ref, done_sem.at[1])
+    energy.start()
+
+    def late(comp):
         return pltpu.make_async_copy(
-            held_ref.at[k], out_ref.at[:, :, k // CUTS, :, columns], sem.at[k]
+            held_ref.at[comp], out_ref.at[pl.ds(GROUP_BINS, GROUP_BINS), :, comp], sem.at[comp]
         )
 
-    for k in range(chunks):
-        rows = mine_ref[:, :, k * cut : (k + 1) * cut].reshape(BLOCKS * ROWS, cut)
-        modes = jnp.dot(coef_ref[...], rows, preferred_element_type=jnp.float32)
-        modes = modes.astype(jnp.bfloat16)
-        for f in range(BINS):
-            for part in range(2):
-                start = (f * 2 + part) * MODES
-                held_ref[k, f, part] = modes[start : start + MODES]
-        put(k).start()
-    energy_out_ref[...] = energy_ref[...]
-    for k in range(chunks):
-        put(k).wait()
+    for comp in range(COMPS):
+
+        def put(f, part, half, rows):
+            held_ref[comp, f, part, :, pl.ds(half * half_points, half_points)] = rows
+
+        group_modes(coef_ref[...], mine_ref, pl.ds(comp * half_points, half_points), put)
+        late(comp).start()
+    for comp in range(COMPS):
+        late(comp).wait()
+    early.wait()
+    energy.wait()
 
 
 def local(snapshots, space_count):
     points = snapshots.shape[3]
-    cut = points // CUTS
-    width = COMPS * points
-    pieces = len([w for widths in chunk_widths(points) for w in widths])
+    width = COMPS * points // GROUPS
+    pieces = len(chunk_plan(points)[1])
     series = jnp.transpose(snapshots, (0, 2, 1, 3)).reshape(COMPS, STEPS, points)
     vmem = pl.BlockSpec(memory_space=pltpu.VMEM)
     hbm = pl.BlockSpec(memory_space=pltpu.HBM)
-    mine, coef, energies = pl.pallas_call(
-        functools.partial(spectra_kernel, points, float(width * space_count)),
+    mine, done, coef, energies = pl.pallas_call(
+        functools.partial(spectra_kernel, points, float(COMPS * points * space_count)),
         out_shape=(
             pltpu.VMEM((BLOCKS, ROWS, width), jnp.bfloat16),
-            jax.ShapeDtypeStruct((BINS * 2 * MODES, BLOCKS * ROWS), jnp.bfloat16),
-            jax.ShapeDtypeStruct((MODES, BINS), jnp.float32),
+            pltpu.VMEM((GROUP_BINS, 2, COMPS, MODES, points), jnp.bfloat16),
+            pltpu.VMEM((BINS * 2 * MODES, BLOCKS * ROWS), jnp.bfloat16),
+            pltpu.VMEM((MODES, BINS), jnp.float32),
         ),
         in_specs=[hbm, hbm],
-        out_specs=(vmem, vmem, vmem),
+        out_specs=(vmem, vmem, vmem, vmem),
         scratch_shapes=[
             pltpu.VMEM((STEPS, STEPS), jnp.float32),
             pltpu.VMEM((STEPS, STEPS), jnp.bfloat16),
-            pltpu.VMEM((2, STEPS, points), jnp.bfloat16),
+            pltpu.VMEM((2, GROUPS, STEPS, points // GROUPS), jnp.bfloat16),
+            pltpu.VMEM((GROUPS, BLOCKS, ROWS, width), jnp.bfloat16),
             pltpu.VMEM((BLOCKS, ROWS, width), jnp.bfloat16),
             pltpu.VMEM((BLOCKS * ROWS, BLOCKS * ROWS), jnp.float32),
-            pltpu.VMEM((SIDE * SIDE, BLOCKS, BLOCKS * ROWS), jnp.float32),
+            pltpu.VMEM((GROUPS, SIDE * SIDE, BLOCKS, LANES), jnp.float32),
             pltpu.VMEM((2, BLOCKS, BLOCKS, LANES), jnp.float32),
             pltpu.VMEM((2, BINS * 2 * MODES, LANES), jnp.float32),
             pltpu.SemaphoreType.DMA,
-            pltpu.SemaphoreType.DMA((2,)),
+            pltpu.SemaphoreType.DMA((2, GROUPS)),
             pltpu.SemaphoreType.DMA((pieces, BLOCKS)),
             pltpu.SemaphoreType.DMA((pieces, BLOCKS)),
-            pltpu.SemaphoreType.DMA((SIDE * SIDE,)),
-            pltpu.SemaphoreType.DMA((SIDE * SIDE,)),
+            pltpu.SemaphoreType.DMA((GROUPS, SIDE * SIDE)),
+            pltpu.SemaphoreType.DMA((GROUPS, SIDE * SIDE)),
             pltpu.SemaphoreType.REGULAR((LEVELS // 2 - 1, 2)),
             pltpu.SemaphoreType.REGULAR((4,)),
         ],
@@ -423,20 +489,21 @@
             jax.ShapeDtypeStruct((BINS, 2, COMPS, MODES, points), jnp.bfloat16),
             jax.ShapeDtypeStruct((MODES, BINS), jnp.float32),
         ),
-        in_specs=[vmem, vmem, vmem],
-        out_specs=(hbm, vmem),
+        in_specs=[vmem, vmem, vmem, vmem],
+        out_specs=(hbm, hbm),
         scratch_shapes=[
-            pltpu.VMEM((COMPS * CUTS, BINS, 2, MODES, cut), jnp.bfloat16),
-            pltpu.SemaphoreType.DMA((COMPS * CUTS,)),
+            pltpu.VMEM((COMPS, GROUP_BINS, 2, MODES, points), jnp.bfloat16),
+            pltpu.SemaphoreType.DMA((COMPS,)),
+            pltpu.SemaphoreType.DMA((2,)),
         ],
-        compiler_params=pltpu.CompilerParams(vmem_limit_bytes=VMEM_BYTES),
+        compiler_params=pltpu.CompilerParams(vmem_limit_bytes=MODES_VMEM_BYTES),
         cost_estimate=pl.CostEstimate(
             flops=4 * STEPS * BINS * 2 * MODES * COMPS * points,
             bytes_accessed=2 * STEPS * COMPS * points,
             transcendentals=0,
         ),
         name="modes_product",
-    )(coef, mine, energies)
+    )(coef, mine, done, energies)
     return jnp.transpose(modes, (0, 1, 3, 2, 4)), energies.T
 
 

time: 245 us -> 245 us (level)
  no operation moved by 1% of the time
where the time goes in v5:
time: 245 us; the launch traced here: 243 us
  Pallas kernels  243 us (99%)
    pallas_call x1, Pallas kernels, local(): pl.pallas_call(functools.partial(spectra_kernel, points, float(COMPS * po...  241 us

profile of v5, /device:TPU:32, one launch (start us, length us, event | category | flops | bytes accessed | tf_op | source)
XLA Modules:
  0.0 243.3 jit_solution(16363072260746358000)
XLA Ops:
  0.6 240.8 %spectra_exchange.1 = (bf16[16,16,9984]{2,1,0:T(8,128)(2,1)S(1)}, bf16[4,2,3,4,6656]{4,3,2,1,0:T(4,128)(2,1)S(1)}, bf16[64,256]{1,0:T(8,128)(2,1)S(1)}, f32[4,8]{1,0:T(4,128)S(1)}) custom-call(f32[256,256]{1,0:T(8,128)} %constant.2.clone.table_ref, bf16[3,256,6656]{2,1,0:T(8,128)(2,1)} %bitcast.5), custom_call_target="tpu_custom_call" | custom-call | flops 5234491392 | bytes 10223616 | tf_op jit(solution)/shard_map/spectra_exchange/pallas_call | solution.py:447
  241.5 1.8 modes_product.1

commit v6 on v5

--- a/solution.py
+++ b/solution.py
@@ -42,10 +42,10 @@
 
 def chunk_plan(points):
     half = points // GROUPS
-    first, second, last = 2 * LANES, 8 * LANES, 8 * LANES
+    first, second, last = 4 * LANES, 20 * LANES, 8 * LANES
     made = [(0, 0, first), (0, first, second - first), (0, second, half - second)]
-    sent = [(0, start, width) for _, start, width in made] + [(0, half, (COMPS - 1) * half)]
     made += [(c, 0, half) for c in range(1, COMPS)]
+    sent = [(0, 0, first), (0, first, second - first), (0, second, COMPS * half - second)]
     sent += [(1, 0, COMPS * half - last), (1, COMPS * half - last, last)]
     return made, sent
 
@@ -320,17 +320,14 @@
         if r == 0:
             signal(plane_sem.at[0], space=plane(0, SIDE - 1))
             make(1)
-    for dz, dc in peers:
-        send(1, dz, dc).start()
-    make(2)
-    for dz, dc in peers:
-        send(2, dz, dc).start()
+        for dz, dc in ring:
+            send(1, dz, dc).start()
     pl.semaphore_wait(plane_sem.at[0], 1)
     signal(plane_sem.at[1], space=plane(1, 0))
     signal(plane_sem.at[2], space=plane(SIDE - 1, 0))
-    for k in range(3, len(made)):
+    for k in range(2, len(made)):
         make(k)
-    for k in range(3, len(sent)):
+    for k in range(2, len(sent)):
         for dz, dc in peers:
             send(k, dz, dc).start()
     pl.semaphore_wait(plane_sem.at[1], 1)
@@ -338,10 +335,12 @@
     signal(plane_sem.at[3], space=plane(SIDE - 1, 0))
     pl.semaphore_wait(plane_sem.at[3], 1)
 
-    others = range(1, SIDE * SIDE)
-
-    def exchange(group, d, arriving):
-        other = lax.rem(here + d, SIDE * SIDE)
+    hops = (0, 1, 2, 1)
+    others = [(dy, dx) for dy in range(SIDE) for dx in range(SIDE)][1:]
+    others.sort(key=lambda step: -hops[step[0]] - hops[step[1]])
+
+    def exchange(group, step, arriving):
+        other = plane(*step)
         slot = other if arriving else here
         return pltpu.make_async_remote_copy(
             src_ref=packed_ref.at[group, here],
@@ -372,7 +371,7 @@
         for d in others:
             exchange(group, d, True).wait_recv()
         packed = packed_ref[group, 0]
-        for s in others:
+        for s in range(1, SIDE * SIDE):
             packed = packed + packed_ref[group, s]
         vec_real, vec_imag, energies = leading_modes(packed / scale, gram_ref)
         coef = coefficient_matrix(vec_real, vec_imag, energies, order_ref)

time: 245 us -> 243 us (level)
  no operation moved by 1% of the time
where the time goes in v6:
time: 243 us; the launch traced here: 241 us
  Pallas kernels  241 us (99%)
    pallas_call x1, Pallas kernels, local(): pl.pallas_call(functools.partial(spectra_kernel, points, float(COMPS * po...  239 us

profile of v6, /device:TPU:32, one launch (start us, length us, event | category | flops | bytes accessed | tf_op | source)
XLA Modules:
  0.0 241.2 jit_solution(8161314146530625070)
XLA Ops:
  0.6 238.8 %spectra_exchange.1 = (bf16[16,16,9984]{2,1,0:T(8,128)(2,1)S(1)}, bf16[4,2,3,4,6656]{4,3,2,1,0:T(4,128)(2,1)S(1)}, bf16[64,256]{1,0:T(8,128)(2,1)S(1)}, f32[4,8]{1,0:T(4,128)S(1)}) custom-call(f32[256,256]{1,0:T(8,128)} %constant.2.clone.table_ref, bf16[3,256,6656]{2,1,0:T(8,128)(2,1)} %bitcast.5), custom_call_target="tpu_custom_call" | custom-call | flops 5234491392 | bytes 10223616 | tf_op jit(solution)/shard_map/spectra_exchange/pallas_call | solution.py:446
  239.4 1.8 modes_product.1

commit v7 on v6

--- a/solution.py
+++ b/solution.py
@@ -257,21 +257,21 @@
         return pltpu.make_async_remote_copy(
             src_ref=made_ref.at[group, to, :, pl.ds(start, width)],
             dst_ref=lands[group].at[me, :, pl.ds(start, width)],
-            send_sem=send_sem.at[k, to],
-            recv_sem=recv_sem.at[k, me],
+            send_sem=send_sem.at[k],
+            recv_sem=recv_sem.at[k],
             device_id={"tblock": to},
             device_id_type=MESH,
         )
 
-    def arrival(k, dz, dc):
+    def whole(k):
         group, start, width = sent[k]
-        sender = peer(dz, dc)
+        part = lands[group].at[pl.ds(0, BLOCKS - 1), :, pl.ds(start, width)]
         return pltpu.make_async_remote_copy(
-            src_ref=made_ref.at[group, sender, :, pl.ds(start, width)],
-            dst_ref=lands[group].at[sender, :, pl.ds(start, width)],
-            send_sem=send_sem.at[k, sender],
-            recv_sem=recv_sem.at[k, sender],
-            device_id={"tblock": sender},
+            src_ref=part,
+            dst_ref=part,
+            send_sem=send_sem.at[k],
+            recv_sem=recv_sem.at[k],
+            device_id={"tblock": peer(1, 0)},
             device_id_type=MESH,
         )
 
@@ -339,15 +339,24 @@
     others = [(dy, dx) for dy in range(SIDE) for dx in range(SIDE)][1:]
     others.sort(key=lambda step: -hops[step[0]] - hops[step[1]])
 
-    def exchange(group, step, arriving):
-        other = plane(*step)
-        slot = other if arriving else here
+    def exchange(group, step):
         return pltpu.make_async_remote_copy(
             src_ref=packed_ref.at[group, here],
-            dst_ref=packed_ref.at[group, slot],
-            send_sem=sum_send_sem.at[group, other],
-            recv_sem=sum_recv_sem.at[group, slot],
-            device_id={"space": other},
+            dst_ref=packed_ref.at[group, here],
+            send_sem=sum_send_sem.at[group],
+            recv_sem=sum_recv_sem.at[group],
+            device_id={"space": plane(*step)},
+            device_id_type=MESH,
+        )
+
+    def whole_exchange(group):
+        part = packed_ref.at[group, pl.ds(0, SIDE * SIDE - 1)]
+        return pltpu.make_async_remote_copy(
+            src_ref=part,
+            dst_ref=part,
+            send_sem=sum_send_sem.at[group],
+            recv_sem=sum_recv_sem.at[group],
+            device_id={"space": plane(0, 1)},
             device_id_type=MESH,
         )
 
@@ -357,8 +366,7 @@
             owner, start, width = sent[k]
             if owner != group:
                 continue
-            for dz, dc in peers:
-                arrival(k, dz, dc).wait_recv()
+            whole(k).wait_recv()
             rows = lands[group][:, :, pl.ds(start, width)].reshape(BLOCKS * ROWS, width)
             part = lax.dot_general(
                 rows, rows, (((1,), (1,)), ((), ())), preferred_element_type=jnp.float32
@@ -367,9 +375,11 @@
             opened = True
         packed_ref[group, here] = pack_gram(total_ref[...])
         for d in others:
-            exchange(group, d, False).start()
-        for d in others:
-            exchange(group, d, True).wait_recv()
+            exchange(group, d).start()
+        for k in range(len(sent)):
+            if sent[k][0] == group:
+                whole(k).wait_send()
+        whole_exchange(group).wait_recv()
         packed = packed_ref[group, 0]
         for s in range(1, SIDE * SIDE):
             packed = packed + packed_ref[group, s]
@@ -389,6 +399,7 @@
         energy_ref[:, columns] = narrow[:, columns]
 
     coef, spread = solve(0)
+    whole_exchange(0).wait_send()
     settle(0, spread)
     for comp in range(COMPS):
 
@@ -401,12 +412,7 @@
     coef_ref[...] = coef
     settle(1, spread)
 
-    for k in range(len(sent)):
-        for dz, dc in peers:
-            send(k, dz, dc).wait_send()
-    for group in range(GROUPS):
-        for d in others:
-            exchange(group, d, False).wait_send()
+    whole_exchange(1).wait_send()
 
 
 def modes_kernel(
@@ -465,10 +471,10 @@
             pltpu.VMEM((2, BINS * 2 * MODES, LANES), jnp.float32),
             pltpu.SemaphoreType.DMA,
             pltpu.SemaphoreType.DMA((2, GROUPS)),
-            pltpu.SemaphoreType.DMA((pieces, BLOCKS)),
-            pltpu.SemaphoreType.DMA((pieces, BLOCKS)),
-            pltpu.SemaphoreType.DMA((GROUPS, SIDE * SIDE)),
-            pltpu.SemaphoreType.DMA((GROUPS, SIDE * SIDE)),
+            pltpu.SemaphoreType.DMA((pieces,)),
+            pltpu.SemaphoreType.DMA((pieces,)),
+            pltpu.SemaphoreType.DMA((GROUPS,)),
+            pltpu.SemaphoreType.DMA((GROUPS,)),
             pltpu.SemaphoreType.REGULAR((LEVELS // 2 - 1, 2)),
             pltpu.SemaphoreType.REGULAR((4,)),
         ],

time: 243 us -> 241 us (level)
  no operation moved by 1% of the time
where the time goes in v7:
time: 241 us; the launch traced here: 239 us
  Pallas kernels  239 us (99%)
    pallas_call x1, Pallas kernels, local(): pl.pallas_call(functools.partial(spectra_kernel, points, float(COMPS * po...  237 us

profile of v7, /device:TPU:32, one launch (start us, length us, event | category | flops | bytes accessed | tf_op | source)
XLA Modules:
  0.0 239.2 jit_solution(8327555281388093076)
XLA Ops:
  0.6 236.7 %spectra_exchange.1 = (bf16[16,16,9984]{2,1,0:T(8,128)(2,1)S(1)}, bf16[4,2,3,4,6656]{4,3,2,1,0:T(4,128)(2,1)S(1)}, bf16[64,256]{1,0:T(8,128)(2,1)S(1)}, f32[4,8]{1,0:T(4,128)S(1)}) custom-call(f32[256,256]{1,0:T(8,128)} %constant.2.clone.table_ref, bf16[3,256,6656]{2,1,0:T(8,128)(2,1)} %bitcast.5), custom_call_target="tpu_custom_call" | custom-call | flops 5234491392 | bytes 10223616 | tf_op jit(solution)/shard_map/spectra_exchange/pallas_call | solution.py:452
  237.4 1.8 modes_product.1

commit v8 on v7

--- a/solution.py
+++ b/solution.py
@@ -20,6 +20,7 @@
 GROUP_BINS = BINS // GROUPS
 GROUP_ROWS = ROWS // GROUPS
 LEVELS = 8
+MARGIN = 8
 SIDE = 4
 LANES = 128
 MESH = pl.DeviceIdType.MESH
@@ -176,7 +177,8 @@
         for half in range(2):
             piece = turned[ROWS * j : ROWS * (j + 1), half * LANES : (half + 1) * LANES]
             order_ref[half, pl.ds(j, ROWS, stride=MODES), :] = piece
-    return jnp.concatenate([order_ref[0], order_ref[1]], axis=1).astype(jnp.bfloat16)
+    ordered = [order_ref[half, : MODES * ROWS] for half in range(2)]
+    return jnp.concatenate(ordered, axis=1).astype(jnp.bfloat16)
 
 
 def group_modes(coef, mine_ref, columns, put):
@@ -360,7 +362,9 @@
             device_id_type=MESH,
         )
 
-    def solve(group):
+    lane = lax.broadcasted_iota(jnp.int32, (MODES, LANES), 1)
+
+    def gram(group):
         opened = False
         for k in range(len(sent)):
             owner, start, width = sent[k]
@@ -373,21 +377,6 @@
             )
             total_ref[...] = total_ref[...] + part if opened else part
             opened = True
-        packed_ref[group, here] = pack_gram(total_ref[...])
-        for d in others:
-            exchange(group, d).start()
-        for k in range(len(sent)):
-            if sent[k][0] == group:
-                whole(k).wait_send()
-        whole_exchange(group).wait_recv()
-        packed = packed_ref[group, 0]
-        for s in range(1, SIDE * SIDE):
-            packed = packed + packed_ref[group, s]
-        vec_real, vec_imag, energies = leading_modes(packed / scale, gram_ref)
-        coef = coefficient_matrix(vec_real, vec_imag, energies, order_ref)
-        return coef, jnp.concatenate(energies, axis=0)
-
-    lane = lax.broadcasted_iota(jnp.int32, (MODES, LANES), 1)
 
     def settle(group, spread):
         narrow = spread
@@ -398,28 +387,59 @@
         columns = slice(group * GROUP_BINS, (group + 1) * GROUP_BINS)
         energy_ref[:, columns] = narrow[:, columns]
 
-    coef, spread = solve(0)
-    whole_exchange(0).wait_send()
-    settle(0, spread)
-    for comp in range(COMPS):
-
-        def put(f, part, half, rows):
-            done_ref[f, part, comp, :, pl.ds(half * half_points, half_points)] = rows
-
-        group_modes(coef, early_ref, pl.ds(comp * half_points, half_points), put)
-
-    coef, spread = solve(1)
-    coef_ref[...] = coef
-    settle(1, spread)
-
-    whole_exchange(1).wait_send()
+    def solve(group, carry):
+        for fixed in range(GROUPS):
+
+            @pl.when(group == fixed)
+            def _():
+                gram(fixed)
+
+        packed_ref[group, here] = pack_gram(total_ref[...])
+        for d in others:
+            exchange(group, d).start()
+        for fixed in range(GROUPS):
+
+            @pl.when(group == fixed)
+            def _():
+                for k in range(len(sent)):
+                    if sent[k][0] == fixed:
+                        whole(k).wait_send()
+
+        whole_exchange(group).wait_recv()
+        packed = packed_ref[group, 0]
+        for s in range(1, SIDE * SIDE):
+            packed = packed + packed_ref[group, s]
+        vec_real, vec_imag, energies = leading_modes(packed / scale, gram_ref)
+        coef_ref[...] = coefficient_matrix(vec_real, vec_imag, energies, order_ref)
+        spread = jnp.concatenate(energies, axis=0)
+        whole_exchange(group).wait_send()
+        for fixed in range(GROUPS):
+
+            @pl.when(group == fixed)
+            def _():
+                settle(fixed, spread)
+
+        @pl.when(group == 0)
+        def _():
+            for comp in range(COMPS):
+
+                def put(f, part, half, rows):
+                    done_ref[f, part, comp, :, pl.ds(half * half_points, half_points)] = rows
+
+                columns = pl.ds(comp * half_points, half_points)
+                group_modes(coef_ref[...], early_ref, columns, put)
+
+        return carry
+
+    lax.fori_loop(0, GROUPS, solve, 0)
 
 
 def modes_kernel(
     coef_ref, mine_ref, done_ref, energy_ref, out_ref, energy_out_ref, held_ref, sem, done_sem
 ):
     half_points = held_ref.shape[4] // GROUPS
-    early = pltpu.make_async_copy(done_ref, out_ref.at[pl.ds(0, GROUP_BINS)], done_sem.at[0])
+    first = pl.ds(0, GROUP_BINS)
+    early = pltpu.make_async_copy(done_ref.at[first], out_ref.at[first], done_sem.at[0])
     early.start()
     energy = pltpu.make_async_copy(energy_ref, energy_out_ref, done_sem.at[1])
     energy.start()
@@ -453,7 +473,7 @@
         functools.partial(spectra_kernel, points, float(COMPS * points * space_count)),
         out_shape=(
             pltpu.VMEM((BLOCKS, ROWS, width), jnp.bfloat16),
-            pltpu.VMEM((GROUP_BINS, 2, COMPS, MODES, points), jnp.bfloat16),
+            pltpu.VMEM((GROUP_BINS + 1, 2, COMPS, MODES, points), jnp.bfloat16),
             pltpu.VMEM((BINS * 2 * MODES, BLOCKS * ROWS), jnp.bfloat16),
             pltpu.VMEM((MODES, BINS), jnp.float32),
         ),
@@ -468,7 +488,7 @@
             pltpu.VMEM((BLOCKS * ROWS, BLOCKS * ROWS), jnp.float32),
             pltpu.VMEM((GROUPS, SIDE * SIDE, BLOCKS, LANES), jnp.float32),
             pltpu.VMEM((2, BLOCKS, BLOCKS, LANES), jnp.float32),
-            pltpu.VMEM((2, BINS * 2 * MODES, LANES), jnp.float32),
+            pltpu.VMEM((2, BINS * 2 * MODES + MARGIN, LANES), jnp.float32),
             pltpu.SemaphoreType.DMA,
             pltpu.SemaphoreType.DMA((2, GROUPS)),
             pltpu.SemaphoreType.DMA((pieces,)),
@@ -497,7 +517,7 @@
         in_specs=[vmem, vmem, vmem, vmem],
         out_specs=(hbm, hbm),
         scratch_shapes=[
-            pltpu.VMEM((COMPS, GROUP_BINS, 2, MODES, points), jnp.bfloat16),
+            pltpu.VMEM((COMPS + 1, GROUP_BINS, 2, MODES, points), jnp.bfloat16),
             pltpu.SemaphoreType.DMA((COMPS,)),
             pltpu.SemaphoreType.DMA((2,)),
         ],

time: 241 us -> 241 us (level)
  no operation moved by 1% of the time
where the time goes in v8:
time: 241 us; the launch traced here: 239 us
  Pallas kernels  238 us (99%)
    pallas_call x1, Pallas kernels, local(): pl.pallas_call(functools.partial(spectra_kernel, points, float(COMPS * po...  236 us

profile of v8, /device:TPU:32, one launch (start us, length us, event | category | flops | bytes accessed | tf_op | source)
XLA Modules:
  0.0 238.9 jit_solution(6638409149073819725)
XLA Ops:
  0.6 236.4 %spectra_exchange.1 = (bf16[16,16,9984]{2,1,0:T(8,128)(2,1)S(1)}, bf16[5,2,3,4,6656]{4,3,2,1,0:T(4,128)(2,1)S(1)}, bf16[64,256]{1,0:T(8,128)(2,1)S(1)}, f32[4,8]{1,0:T(4,128)S(1)}) custom-call(f32[256,256]{1,0:T(8,128)} %constant.2.clone.table_ref, bf16[3,256,6656]{2,1,0:T(8,128)(2,1)} %bitcast.5), custom_call_target="tpu_custom_call" | custom-call | flops 5234491392 | bytes 10223616 | tf_op jit(solution)/shard_map/spectra_exchange/pallas_call | solution.py:472
  237.0 1.8 modes_product.1

commit v9 on v8

--- a/solution.py
+++ b/solution.py
@@ -43,7 +43,7 @@
 
 def chunk_plan(points):
     half = points // GROUPS
-    first, second, last = 4 * LANES, 20 * LANES, 8 * LANES
+    first, second, last = 4 * LANES, 24 * LANES, 8 * LANES
     made = [(0, 0, first), (0, first, second - first), (0, second, half - second)]
     made += [(c, 0, half) for c in range(1, COMPS)]
     sent = [(0, 0, first), (0, first, second - first), (0, second, COMPS * half - second)]

time: 241 us -> 241 us (level)
  no operation moved by 1% of the time
where the time goes in v9:
time: 241 us; the launch traced here: 239 us
  Pallas kernels  238 us (99%)
    pallas_call x1, Pallas kernels, local(): pl.pallas_call(functools.partial(spectra_kernel, points, float(COMPS * po...  237 us

profile of v9, /device:TPU:32, one launch (start us, length us, event | category | flops | bytes accessed | tf_op | source)
XLA Modules:
  0.0 239.0 jit_solution(4711965376323078083)
XLA Ops:
  0.6 236.5 %spectra_exchange.1 = (bf16[16,16,9984]{2,1,0:T(8,128)(2,1)S(1)}, bf16[5,2,3,4,6656]{4,3,2,1,0:T(4,128)(2,1)S(1)}, bf16[64,256]{1,0:T(8,128)(2,1)S(1)}, f32[4,8]{1,0:T(4,128)S(1)}) custom-call(f32[256,256]{1,0:T(8,128)} %constant.2.clone.table_ref, bf16[3,256,6656]{2,1,0:T(8,128)(2,1)} %bitcast.5), custom_call_target="tpu_custom_call" | custom-call | flops 5234491392 | bytes 10223616 | tf_op jit(solution)/shard_map/spectra_exchange/pallas_call | solution.py:472
  237.2 1.8 modes_product.1
